TPU v7x, 128 devices: a whole 4x4x4 slice. The times are simulated.
128 devices in a mesh: net: 16 (over y, x), line: 8 (over z, core).
Axes of the slice: x: 4, y: 4, z: 4, core: 2. Of those that a mesh axis runs over, the one named last changes fastest.
Arguments:
- inverses: float32 [512, 1024, 1024], P('net', 'line'), as said below
- node_counts: int32 [512], P('net'), may hold values from 384 to 1024, as said below
- sources: float32 [16, 512, 1024], P(None, 'net'), may hold values from -6 to 6
- port_slot: int32 [512, 64], P('net', 'line'), may hold values from 0 to 1023, as said below
- end_slot: int32 [2, 16384], P(None, ('net', 'line')), may hold values from 0 to 1023, as said below
- modal_map: float32 [6, 6, 16384], P(None, None, ('net', 'line')), may hold values from -1 to 1
- delay_steps: int32 [6, 16384], P(None, ('net', 'line')), may hold values from 1 to 64
- wave_buffer: float32 [2, 6, 64, 16384], P(None, None, None, ('net', 'line')), may hold values from -6 to 6
- yc_decay: float32 [6, 30, 16384], P(None, None, ('net', 'line')), may hold values from 0.2 to 0.99
- yc_residue: float32 [6, 30, 16384], P(None, None, ('net', 'line')), may hold values from -0.04 to 0.04
- yc_direct: float32 [6, 16384], P(None, ('net', 'line')), may hold values from 0.25 to 1
- yc_state: float32 [2, 6, 30, 16384], P(None, None, None, ('net', 'line')), may hold values from -0.6 to 0.6
- prop_decay: float32 [6, 30, 16384], P(None, None, ('net', 'line')), may hold values from 0.2 to 0.99
- prop_residue: float32 [6, 30, 16384], P(None, None, ('net', 'line')), may hold values from 0 to 0.008
- prop_state: float32 [2, 6, 30, 16384], P(None, None, None, ('net', 'line')), may hold values from -0.6 to 0.6
Outputs:
- node_volts: float32 [16, 512, 1024], P(None, 'net', 'line')
- line_currents: float32 [16, 2, 6, 16384], P(None, None, None, ('net', 'line'))
Inputs may be any that keep to these rules, and one draw needn't show every extreme that they name: `inverses`: rows and columns at and past node_counts of a subnetwork are zero. `node_counts`: some subnetwork has 1024 nodes and some has 384. port_slot // 8 is the device along net+line that holds the joined line end and port_slot % 8 a slot; the ports held by one device name distinct values, and in every draw some device fills all 8 slots of some other device. end_slot // 8 is the device along net+line that holds the joined port and end_slot % 8 the same slot; the line ends held by one device name distinct values, and in every draw some device receives 8 of them from one other device.
All inputs are finite; a program needn't handle non-finite values.
Results may differ from a plain program's by a relative error of at most 0.0001.
Values sent between devices are 32-bit elements; how exact they have to be, the bound alone decides.
A program may use at most 64 MiB of HBM per device.

v0:
```python
import jax
import jax.numpy as jnp
from jax import lax
from jax.sharding import PartitionSpec as P


def read_delayed(extended, delay_steps, step_index, buffer_len):
    read_at = buffer_len + step_index - delay_steps
    depth = jnp.arange(extended.shape[2], dtype=jnp.int32)
    picker = (depth[None, :, None] == read_at[:, None, :]).astype(extended.dtype)
    return jnp.sum(extended * picker[None], axis=2)


def move_back(outgoing):
    returned = lax.all_to_all(outgoing, ("net", "line"), split_axis=1, concat_axis=1, tiled=True)
    return returned


def move_forward(sending):
    arrived = lax.all_to_all(sending, ("net", "line"), split_axis=1, concat_axis=1, tiled=True)
    return arrived


def body(
    inverses,
    node_counts,
    sources,
    port_slot,
    end_slot,
    modal_map,
    delay_steps,
    wave_buffer,
    yc_decay,
    yc_residue,
    yc_direct,
    yc_state,
    prop_decay,
    prop_residue,
    prop_state,
):
    net_size = lax.axis_size("net")
    line_size = lax.axis_size("line")
    device_count = net_size * line_size
    sub_count, row_count, node_total = inverses.shape
    step_count = sources.shape[0]
    port_cols = port_slot.shape[1]
    mode_count = modal_map.shape[0]
    line_count = end_slot.shape[1]
    buffer_len = wave_buffer.shape[2]
    port_total = port_cols * line_size
    slot_cap = max(2, 4 * sub_count * port_cols // device_count)
    slot_width = device_count * slot_cap
    line_pos = lax.axis_index("line")
    row_ids = line_pos * row_count + jnp.arange(row_count, dtype=jnp.int32)
    live_mask = row_ids[None, :] < node_counts[:, None]
    port_flat = port_slot.reshape(-1)
    end_flat = end_slot.reshape(-1)
    used_nodes = port_total * mode_count
    first_port = line_pos * port_cols
    extended = jnp.concatenate(
        [wave_buffer, jnp.zeros((2, mode_count, step_count, line_count), jnp.float32)], axis=2
    )
    volts_init = jnp.zeros((step_count, sub_count, row_count), jnp.float32)
    currents_init = jnp.zeros((step_count, 2, mode_count, line_count), jnp.float32)

    def advance(step_index, carried):
        yc_now, prop_now, extended, volts_acc, currents_acc = carried
        delayed = read_delayed(extended, delay_steps, step_index, buffer_len)
        prop_now = prop_decay[None] * prop_now + prop_residue[None] * delayed[::-1][:, :, None, :]
        history = jnp.sum(prop_now, axis=2)
        history_phase = jnp.sum(modal_map[None] * history[:, None], axis=2)
        outgoing = (
            jnp.zeros((mode_count, slot_width), jnp.float32)
            .at[:, end_flat]
            .set(history_phase.transpose(1, 0, 2).reshape(mode_count, 2 * line_count))
        )
        returned = move_back(outgoing)
        own_ports = (
            returned[:, port_flat]
            .reshape(mode_count, sub_count, port_cols)
            .transpose(1, 2, 0)
            .reshape(sub_count, port_cols * mode_count)
        )
        port_currents = lax.all_gather(own_ports, "line", axis=1, tiled=True)
        port_currents = (
            port_currents.reshape(sub_count, port_total, mode_count)
            .transpose(0, 2, 1)
            .reshape(sub_count, used_nodes)
        )
        source_now = lax.dynamic_index_in_dim(sources, step_index, 0, keepdims=False)
        injection = source_now + jnp.pad(port_currents, ((0, 0), (0, node_total - used_nodes)))
        solved = jnp.einsum("src,sc->sr", inverses, injection, precision=lax.Precision.HIGHEST)
        solved = jnp.where(live_mask, solved, 0.0)
        gathered = lax.all_gather(solved, "line", axis=1, tiled=True)
        by_mode = gathered[:, :used_nodes].reshape(sub_count, mode_count, port_total)
        own_volts = lax.dynamic_slice_in_dim(by_mode, first_port, port_cols, 2)
        own_volts = own_volts.transpose(1, 0, 2).reshape(mode_count, sub_count * port_cols)
        sending = jnp.zeros((mode_count, slot_width), jnp.float32).at[:, port_flat].set(own_volts)
        arrived = move_forward(sending)
        end_volts = arrived[:, end_flat].reshape(mode_count, 2, line_count)
        modal_volts = jnp.sum(modal_map[:, :, None, :] * end_volts[:, None], axis=0).transpose(
            1, 0, 2
        )
        yc_now = yc_decay[None] * yc_now + yc_residue[None] * modal_volts[:, :, None, :]
        charac = yc_direct[None] * modal_volts + jnp.sum(yc_now, axis=2)
        current = charac - history
        wave_out = 2.0 * charac - history
        extended = lax.dynamic_update_slice_in_dim(
            extended, wave_out[:, :, None, :], buffer_len + step_index, 2
        )
        volts_acc = lax.dynamic_update_slice_in_dim(volts_acc, solved[None], step_index, 0)
        currents_acc = lax.dynamic_update_slice_in_dim(currents_acc, current[None], step_index, 0)
        return (yc_now, prop_now, extended, volts_acc, currents_acc)

    final = lax.fori_loop(
        0, step_count, advance, (yc_state, prop_state, extended, volts_init, currents_init)
    )
    return (final[3], final[4])


def solution(mesh):
    placed = (
        P("net", "line", None),
        P("net"),
        P(None, "net", None),
        P("net", "line"),
        P(None, ("net", "line")),
        P(None, None, ("net", "line")),
        P(None, ("net", "line")),
        P(None, None, None, ("net", "line")),
        P(None, None, ("net", "line")),
        P(None, None, ("net", "line")),
        P(None, ("net", "line")),
        P(None, None, None, ("net", "line")),
        P(None, None, ("net", "line")),
        P(None, None, ("net", "line")),
        P(None, None, None, ("net", "line")),
    )
    return jax.shard_map(
        body,
        mesh=mesh,
        in_specs=placed,
        out_specs=(P(None, "net", "line"), P(None, None, None, ("net", "line"))),
        check_vma=False,
    )
```

profile of v0, /device:TPU:1, one launch (start us, length us, event | category | flops | bytes accessed | tf_op | source)
XLA Modules:
  0.0 1480.3 jit_solution(7146146301842330971)
XLA Ops:
  4.8 1475.5 %while.24 = (s32[]{:T(128)}, f32[2,6,30,128]{3,0,2,1:T(2,128)S(1)}, f32[2,6,30,128]{3,0,2,1:T(2,128)S(1)}, f32[2,6,80,128]{3,0,1,2:T(2,128)S(1)}, f32[16,32,128]...) while((s32[]{:T(128)}, f32[2,6,30,128]{3,0,2,1:T(2,128)S(1)}, ...), condition=%wide.region_8.9_spmd.clone, body=%wide.region_0.8_spmd.clone.sunk | while | flops 51154176 | bytes 23705212 | solution.py:115
  36.6 13.8 all-gather.3
  52.0 16.4 %fusion.29 = f32[32,1,128]{2,1,0:T(1,128)S(1)} fusion(f32[32,128,1024]{2,1,0:T(8,128)} %get-tuple-element.744, f32[32,1024,1]{1,0,2:T(8,128)S(1)} %fusion.28), kind=kOutput, calls=%fused_computation.16.clone.1 | convolution fusion | flops 50331648 | bytes 16924672 | tf_op jit(solution)/shard_map/while/body/eval_jaxpr/src,sc->sr/dot_general | solution.py:92
  113.8 13.7 all-to-all-done
  128.4 13.8 all-gather.3
  143.8 16.4 %fusion.29 = f32[32,1,128]{2,1,0:T(1,128)S(1)} fusion(f32[32,128,1024]{2,1,0:T(8,128)} %get-tuple-element.744, f32[32,1024,1]{1,0,2:T(8,128)S(1)} %fusion.28), kind=kOutput, calls=%fused_computation.16.clone.1 | convolution fusion | flops 50331648 | bytes 16924672 | tf_op jit(solution)/shard_map/while/body/eval_jaxpr/src,sc->sr/dot_general | solution.py:92
  205.6 13.7 all-to-all-done
  220.2 13.8 all-gather.3
  235.6 16.4 %fusion.29 = f32[32,1,128]{2,1,0:T(1,128)S(1)} fusion(f32[32,128,1024]{2,1,0:T(8,128)} %get-tuple-element.744, f32[32,1024,1]{1,0,2:T(8,128)S(1)} %fusion.28), kind=kOutput, calls=%fused_computation.16.clone.1 | convolution fusion | flops 50331648 | bytes 16924672 | tf_op jit(solution)/shard_map/while/body/eval_jaxpr/src,sc->sr/dot_general | solution.py:92
  297.4 13.7 all-to-all-done
  312.0 13.8 all-gather.3
  327.4 16.4 %fusion.29 = f32[32,1,128]{2,1,0:T(1,128)S(1)} fusion(f32[32,128,1024]{2,1,0:T(8,128)} %get-tuple-element.744, f32[32,1024,1]{1,0,2:T(8,128)S(1)} %fusion.28), kind=kOutput, calls=%fused_computation.16.clone.1 | convolution fusion | flops 50331648 | bytes 16924672 | tf_op jit(solution)/shard_map/while/body/eval_jaxpr/src,sc->sr/dot_general | solution.py:92
  389.2 13.7 all-to-all-done
  403.8 13.8 all-gather.3
  419.2 16.4 %fusion.29 = f32[32,1,128]{2,1,0:T(1,128)S(1)} fusion(f32[32,128,1024]{2,1,0:T(8,128)} %get-tuple-element.744, f32[32,1024,1]{1,0,2:T(8,128)S(1)} %fusion.28), kind=kOutput, calls=%fused_computation.16.clone.1 | convolution fusion | flops 50331648 | bytes 16924672 | tf_op jit(solution)/shard_map/while/body/eval_jaxpr/src,sc->sr/dot_general | solution.py:92
  481.0 13.7 all-to-all-done
  495.6 13.8 all-gather.3
  511.0 16.4 %fusion.29 = f32[32,1,128]{2,1,0:T(1,128)S(1)} fusion(f32[32,128,1024]{2,1,0:T(8,128)} %get-tuple-element.744, f32[32,1024,1]{1,0,2:T(8,128)S(1)} %fusion.28), kind=kOutput, calls=%fused_computation.16.clone.1 | convolution fusion | flops 50331648 | bytes 16924672 | tf_op jit(solution)/shard_map/while/body/eval_jaxpr/src,sc->sr/dot_general | solution.py:92
  572.8 13.7 all-to-all-done
  587.4 13.8 all-gather.3
  602.8 16.4 %fusion.29 = f32[32,1,128]{2,1,0:T(1,128)S(1)} fusion(f32[32,128,1024]{2,1,0:T(8,128)} %get-tuple-element.744, f32[32,1024,1]{1,0,2:T(8,128)S(1)} %fusion.28), kind=kOutput, calls=%fused_computation.16.clone.1 | convolution fusion | flops 50331648 | bytes 16924672 | tf_op jit(solution)/shard_map/while/body/eval_jaxpr/src,sc->sr/dot_general | solution.py:92
  664.6 13.7 all-to-all-done
  679.2 13.8 all-gather.3
  694.6 16.4 %fusion.29 = f32[32,1,128]{2,1,0:T(1,128)S(1)} fusion(f32[32,128,1024]{2,1,0:T(8,128)} %get-tuple-element.744, f32[32,1024,1]{1,0,2:T(8,128)S(1)} %fusion.28), kind=kOutput, calls=%fused_computation.16.clone.1 | convolution fusion | flops 50331648 | bytes 16924672 | tf_op jit(solution)/shard_map/while/body/eval_jaxpr/src,sc->sr/dot_general | solution.py:92
  756.4 13.7 all-to-all-done
  771.0 13.8 all-gather.3
  786.4 16.4 %fusion.29 = f32[32,1,128]{2,1,0:T(1,128)S(1)} fusion(f32[32,128,1024]{2,1,0:T(8,128)} %get-tuple-element.744, f32[32,1024,1]{1,0,2:T(8,128)S(1)} %fusion.28), kind=kOutput, calls=%fused_computation.16.clone.1 | convolution fusion | flops 50331648 | bytes 16924672 | tf_op jit(solution)/shard_map/while/body/eval_jaxpr/src,sc->sr/dot_general | solution.py:92
  848.2 13.7 all-to-all-done
  862.8 13.8 all-gather.3
  878.2 16.4 %fusion.29 = f32[32,1,128]{2,1,0:T(1,128)S(1)} fusion(f32[32,128,1024]{2,1,0:T(8,128)} %get-tuple-element.744, f32[32,1024,1]{1,0,2:T(8,128)S(1)} %fusion.28), kind=kOutput, calls=%fused_computation.16.clone.1 | convolution fusion | flops 50331648 | bytes 16924672 | tf_op jit(solution)/shard_map/while/body/eval_jaxpr/src,sc->sr/dot_general | solution.py:92
  940.0 13.7 all-to-all-done
  954.6 13.8 all-gather.3
  970.0 16.4 %fusion.29 = f32[32,1,128]{2,1,0:T(1,128)S(1)} fusion(f32[32,128,1024]{2,1,0:T(8,128)} %get-tuple-element.744, f32[32,1024,1]{1,0,2:T(8,128)S(1)} %fusion.28), kind=kOutput, calls=%fused_computation.16.clone.1 | convolution fusion | flops 50331648 | bytes 16924672 | tf_op jit(solution)/shard_map/while/body/eval_jaxpr/src,sc->sr/dot_general | solution.py:92
  1031.8 13.7 all-to-all-done
  1046.4 13.8 all-gather.3
  1061.7 16.4 %fusion.29 = f32[32,1,128]{2,1,0:T(1,128)S(1)} fusion(f32[32,128,1024]{2,1,0:T(8,128)} %get-tuple-element.744, f32[32,1024,1]{1,0,2:T(8,128)S(1)} %fusion.28), kind=kOutput, calls=%fused_computation.16.clone.1 | convolution fusion | flops 50331648 | bytes 16924672 | tf_op jit(solution)/shard_map/while/body/eval_jaxpr/src,sc->sr/dot_general | solution.py:92
  1123.5 13.7 all-to-all-done
  1138.2 13.8 all-gather.3
  1153.5 16.4 %fusion.29 = f32[32,1,128]{2,1,0:T(1,128)S(1)} fusion(f32[32,128,1024]{2,1,0:T(8,128)} %get-tuple-element.744, f32[32,1024,1]{1,0,2:T(8,128)S(1)} %fusion.28), kind=kOutput, calls=%fused_computation.16.clone.1 | convolution fusion | flops 50331648 | bytes 16924672 | tf_op jit(solution)/shard_map/while/body/eval_jaxpr/src,sc->sr/dot_general | solution.py:92
  1215.3 13.7 all-to-all-done
  1230.0 13.8 all-gather.3
  1245.3 16.4 %fusion.29 = f32[32,1,128]{2,1,0:T(1,128)S(1)} fusion(f32[32,128,1024]{2,1,0:T(8,128)} %get-tuple-element.744, f32[32,1024,1]{1,0,2:T(8,128)S(1)} %fusion.28), kind=kOutput, calls=%fused_computation.16.clone.1 | convolution fusion | flops 50331648 | bytes 16924672 | tf_op jit(solution)/shard_map/while/body/eval_jaxpr/src,sc->sr/dot_general | solution.py:92
  1307.1 13.7 all-to-all-done
  1321.8 13.8 all-gather.3
  1337.1 16.4 %fusion.29 = f32[32,1,128]{2,1,0:T(1,128)S(1)} fusion(f32[32,128,1024]{2,1,0:T(8,128)} %get-tuple-element.744, f32[32,1024,1]{1,0,2:T(8,128)S(1)} %fusion.28), kind=kOutput, calls=%fused_computation.16.clone.1 | convolution fusion | flops 50331648 | bytes 16924672 | tf_op jit(solution)/shard_map/while/body/eval_jaxpr/src,sc->sr/dot_general | solution.py:92
  1398.9 13.7 all-to-all-done
  1413.6 13.8 all-gather.3
  1428.9 16.4 %fusion.29 = f32[32,1,128]{2,1,0:T(1,128)S(1)} fusion(f32[32,128,1024]{2,1,0:T(8,128)} %get-tuple-element.744, f32[32,1024,1]{1,0,2:T(8,128)S(1)} %fusion.28), kind=kOutput, calls=%fused_computation.16.clone.1 | convolution fusion | flops 50331648 | bytes 16924672 | tf_op jit(solution)/shard_map/while/body/eval_jaxpr/src,sc->sr/dot_general | solution.py:92
  (810 shorter events, 787.6 us)
Async XLA Ops:
  10.6 25.1 %all-to-all-start = ((f32[6,128,8]{0,2,1:T(8,128)}), f32[6,128,8]{0,2,1:T(8,128)S(1)}, u32[]{:S(2)}, u32[]{:S(2)}) async-start(f32[6,128,8]{0,2,1:T(8,128)} %bitcast.98), calls=%async_computation | async-start | bytes 1048576 | tf_op jit(solution)/shard_map/while/body/eval_jaxpr/all_to_all | solution.py:15
  52.0 50.7 %copy-start.3 = (f32[6,128]{1,0:T(8,128)S(1)}, f32[6,128]{1,0:T(8,128)}, u32[]{:S(2)}) copy-start(f32[6,128]{1,0:T(8,128)} %get-tuple-element.746) | copy-start | bytes 9220 | tf_op jit(solution)/shard_map/while
  84.3 17.3 %all-to-all-start.1 = ((f32[6,128,8]{0,2,1:T(8,128)}), f32[6,128,8]{0,2,1:T(8,128)S(1)}, u32[]{:S(2)}, u32[]{:S(2)}) async-start(f32[6,128,8]{0,2,1:T(8,128)} %bitcast.107), calls=%async_computation.1 | async-start | bytes 1048576 | tf_op jit(solution)/shard_map/while/body/eval_jaxpr/all_to_all | solution.py:20
  109.2 18.3 %all-to-all-start = ((f32[6,128,8]{0,2,1:T(8,128)}), f32[6,128,8]{0,2,1:T(8,128)S(1)}, u32[]{:S(2)}, u32[]{:S(2)}) async-start(f32[6,128,8]{0,2,1:T(8,128)} %bitcast.98), calls=%async_computation | async-start | bytes 1048576 | tf_op jit(solution)/shard_map/while/body/eval_jaxpr/all_to_all | solution.py:15
  143.8 50.7 %copy-start.3 = (f32[6,128]{1,0:T(8,128)S(1)}, f32[6,128]{1,0:T(8,128)}, u32[]{:S(2)}) copy-start(f32[6,128]{1,0:T(8,128)} %get-tuple-element.746) | copy-start | bytes 9220 | tf_op jit(solution)/shard_map/while
  176.1 17.3 %all-to-all-start.1 = ((f32[6,128,8]{0,2,1:T(8,128)}), f32[6,128,8]{0,2,1:T(8,128)S(1)}, u32[]{:S(2)}, u32[]{:S(2)}) async-start(f32[6,128,8]{0,2,1:T(8,128)} %bitcast.107), calls=%async_computation.1 | async-start | bytes 1048576 | tf_op jit(solution)/shard_map/while/body/eval_jaxpr/all_to_all | solution.py:20
  201.0 18.3 %all-to-all-start = ((f32[6,128,8]{0,2,1:T(8,128)}), f32[6,128,8]{0,2,1:T(8,128)S(1)}, u32[]{:S(2)}, u32[]{:S(2)}) async-start(f32[6,128,8]{0,2,1:T(8,128)} %bitcast.98), calls=%async_computation | async-start | bytes 1048576 | tf_op jit(solution)/shard_map/while/body/eval_jaxpr/all_to_all | solution.py:15
  235.6 50.7 %copy-start.3 = (f32[6,128]{1,0:T(8,128)S(1)}, f32[6,128]{1,0:T(8,128)}, u32[]{:S(2)}) copy-start(f32[6,128]{1,0:T(8,128)} %get-tuple-element.746) | copy-start | bytes 9220 | tf_op jit(solution)/shard_map/while
  267.9 17.3 %all-to-all-start.1 = ((f32[6,128,8]{0,2,1:T(8,128)}), f32[6,128,8]{0,2,1:T(8,128)S(1)}, u32[]{:S(2)}, u32[]{:S(2)}) async-start(f32[6,128,8]{0,2,1:T(8,128)} %bitcast.107), calls=%async_computation.1 | async-start | bytes 1048576 | tf_op jit(solution)/shard_map/while/body/eval_jaxpr/all_to_all | solution.py:20
  292.8 18.3 %all-to-all-start = ((f32[6,128,8]{0,2,1:T(8,128)}), f32[6,128,8]{0,2,1:T(8,128)S(1)}, u32[]{:S(2)}, u32[]{:S(2)}) async-start(f32[6,128,8]{0,2,1:T(8,128)} %bitcast.98), calls=%async_computation | async-start | bytes 1048576 | tf_op jit(solution)/shard_map/while/body/eval_jaxpr/all_to_all | solution.py:15
  327.4 50.7 %copy-start.3 = (f32[6,128]{1,0:T(8,128)S(1)}, f32[6,128]{1,0:T(8,128)}, u32[]{:S(2)}) copy-start(f32[6,128]{1,0:T(8,128)} %get-tuple-element.746) | copy-start | bytes 9220 | tf_op jit(solution)/shard_map/while
  359.7 17.3 %all-to-all-start.1 = ((f32[6,128,8]{0,2,1:T(8,128)}), f32[6,128,8]{0,2,1:T(8,128)S(1)}, u32[]{:S(2)}, u32[]{:S(2)}) async-start(f32[6,128,8]{0,2,1:T(8,128)} %bitcast.107), calls=%async_computation.1 | async-start | bytes 1048576 | tf_op jit(solution)/shard_map/while/body/eval_jaxpr/all_to_all | solution.py:20
  384.6 18.3 %all-to-all-start = ((f32[6,128,8]{0,2,1:T(8,128)}), f32[6,128,8]{0,2,1:T(8,128)S(1)}, u32[]{:S(2)}, u32[]{:S(2)}) async-start(f32[6,128,8]{0,2,1:T(8,128)} %bitcast.98), calls=%async_computation | async-start | bytes 1048576 | tf_op jit(solution)/shard_map/while/body/eval_jaxpr/all_to_all | solution.py:15
  419.2 50.7 %copy-start.3 = (f32[6,128]{1,0:T(8,128)S(1)}, f32[6,128]{1,0:T(8,128)}, u32[]{:S(2)}) copy-start(f32[6,128]{1,0:T(8,128)} %get-tuple-element.746) | copy-start | bytes 9220 | tf_op jit(solution)/shard_map/while
  451.5 17.3 %all-to-all-start.1 = ((f32[6,128,8]{0,2,1:T(8,128)}), f32[6,128,8]{0,2,1:T(8,128)S(1)}, u32[]{:S(2)}, u32[]{:S(2)}) async-start(f32[6,128,8]{0,2,1:T(8,128)} %bitcast.107), calls=%async_computation.1 | async-start | bytes 1048576 | tf_op jit(solution)/shard_map/while/body/eval_jaxpr/all_to_all | solution.py:20
  476.3 18.3 %all-to-all-start = ((f32[6,128,8]{0,2,1:T(8,128)}), f32[6,128,8]{0,2,1:T(8,128)S(1)}, u32[]{:S(2)}, u32[]{:S(2)}) async-start(f32[6,128,8]{0,2,1:T(8,128)} %bitcast.98), calls=%async_computation | async-start | bytes 1048576 | tf_op jit(solution)/shard_map/while/body/eval_jaxpr/all_to_all | solution.py:15
  511.0 50.7 %copy-start.3 = (f32[6,128]{1,0:T(8,128)S(1)}, f32[6,128]{1,0:T(8,128)}, u32[]{:S(2)}) copy-start(f32[6,128]{1,0:T(8,128)} %get-tuple-element.746) | copy-start | bytes 9220 | tf_op jit(solution)/shard_map/while
  543.3 17.3 %all-to-all-start.1 = ((f32[6,128,8]{0,2,1:T(8,128)}), f32[6,128,8]{0,2,1:T(8,128)S(1)}, u32[]{:S(2)}, u32[]{:S(2)}) async-start(f32[6,128,8]{0,2,1:T(8,128)} %bitcast.107), calls=%async_computation.1 | async-start | bytes 1048576 | tf_op jit(solution)/shard_map/while/body/eval_jaxpr/all_to_all | solution.py:20
  568.1 18.3 %all-to-all-start = ((f32[6,128,8]{0,2,1:T(8,128)}), f32[6,128,8]{0,2,1:T(8,128)S(1)}, u32[]{:S(2)}, u32[]{:S(2)}) async-start(f32[6,128,8]{0,2,1:T(8,128)} %bitcast.98), calls=%async_computation | async-start | bytes 1048576 | tf_op jit(solution)/shard_map/while/body/eval_jaxpr/all_to_all | solution.py:15
  602.8 50.7 %copy-start.3 = (f32[6,128]{1,0:T(8,128)S(1)}, f32[6,128]{1,0:T(8,128)}, u32[]{:S(2)}) copy-start(f32[6,128]{1,0:T(8,128)} %get-tuple-element.746) | copy-start | bytes 9220 | tf_op jit(solution)/shard_map/while
  635.0 17.3 %all-to-all-start.1 = ((f32[6,128,8]{0,2,1:T(8,128)}), f32[6,128,8]{0,2,1:T(8,128)S(1)}, u32[]{:S(2)}, u32[]{:S(2)}) async-start(f32[6,128,8]{0,2,1:T(8,128)} %bitcast.107), calls=%async_computation.1 | async-start | bytes 1048576 | tf_op jit(solution)/shard_map/while/body/eval_jaxpr/all_to_all | solution.py:20
  659.9 18.3 %all-to-all-start = ((f32[6,128,8]{0,2,1:T(8,128)}), f32[6,128,8]{0,2,1:T(8,128)S(1)}, u32[]{:S(2)}, u32[]{:S(2)}) async-start(f32[6,128,8]{0,2,1:T(8,128)} %bitcast.98), calls=%async_computation | async-start | bytes 1048576 | tf_op jit(solution)/shard_map/while/body/eval_jaxpr/all_to_all | solution.py:15
  694.6 50.7 %copy-start.3 = (f32[6,128]{1,0:T(8,128)S(1)}, f32[6,128]{1,0:T(8,128)}, u32[]{:S(2)}) copy-start(f32[6,128]{1,0:T(8,128)} %get-tuple-element.746) | copy-start | bytes 9220 | tf_op jit(solution)/shard_map/while
  726.8 17.3 %all-to-all-start.1 = ((f32[6,128,8]{0,2,1:T(8,128)}), f32[6,128,8]{0,2,1:T(8,128)S(1)}, u32[]{:S(2)}, u32[]{:S(2)}) async-start(f32[6,128,8]{0,2,1:T(8,128)} %bitcast.107), calls=%async_computation.1 | async-start | bytes 1048576 | tf_op jit(solution)/shard_map/while/body/eval_jaxpr/all_to_all | solution.py:20
  751.7 18.3 %all-to-all-start = ((f32[6,128,8]{0,2,1:T(8,128)}), f32[6,128,8]{0,2,1:T(8,128)S(1)}, u32[]{:S(2)}, u32[]{:S(2)}) async-start(f32[6,128,8]{0,2,1:T(8,128)} %bitcast.98), calls=%async_computation | async-start | bytes 1048576 | tf_op jit(solution)/shard_map/while/body/eval_jaxpr/all_to_all | solution.py:15
  786.3 50.7 %copy-start.3 = (f32[6,128]{1,0:T(8,128)S(1)}, f32[6,128]{1,0:T(8,128)}, u32[]{:S(2)}) copy-start(f32[6,128]{1,0:T(8,128)} %get-tuple-element.746) | copy-start | bytes 9220 | tf_op jit(solution)/shard_map/while
  818.6 17.3 %all-to-all-start.1 = ((f32[6,128,8]{0,2,1:T(8,128)}), f32[6,128,8]{0,2,1:T(8,128)S(1)}, u32[]{:S(2)}, u32[]{:S(2)}) async-start(f32[6,128,8]{0,2,1:T(8,128)} %bitcast.107), calls=%async_computation.1 | async-start | bytes 1048576 | tf_op jit(solution)/shard_map/while/body/eval_jaxpr/all_to_all | solution.py:20
  843.5 18.3 %all-to-all-start = ((f32[6,128,8]{0,2,1:T(8,128)}), f32[6,128,8]{0,2,1:T(8,128)S(1)}, u32[]{:S(2)}, u32[]{:S(2)}) async-start(f32[6,128,8]{0,2,1:T(8,128)} %bitcast.98), calls=%async_computation | async-start | bytes 1048576 | tf_op jit(solution)/shard_map/while/body/eval_jaxpr/all_to_all | solution.py:15
  878.1 50.7 %copy-start.3 = (f32[6,128]{1,0:T(8,128)S(1)}, f32[6,128]{1,0:T(8,128)}, u32[]{:S(2)}) copy-start(f32[6,128]{1,0:T(8,128)} %get-tuple-element.746) | copy-start | bytes 9220 | tf_op jit(solution)/shard_map/while
  910.4 17.3 %all-to-all-start.1 = ((f32[6,128,8]{0,2,1:T(8,128)}), f32[6,128,8]{0,2,1:T(8,128)S(1)}, u32[]{:S(2)}, u32[]{:S(2)}) async-start(f32[6,128,8]{0,2,1:T(8,128)} %bitcast.107), calls=%async_computation.1 | async-start | bytes 1048576 | tf_op jit(solution)/shard_map/while/body/eval_jaxpr/all_to_all | solution.py:20
  935.3 18.3 %all-to-all-start = ((f32[6,128,8]{0,2,1:T(8,128)}), f32[6,128,8]{0,2,1:T(8,128)S(1)}, u32[]{:S(2)}, u32[]{:S(2)}) async-start(f32[6,128,8]{0,2,1:T(8,128)} %bitcast.98), calls=%async_computation | async-start | bytes 1048576 | tf_op jit(solution)/shard_map/while/body/eval_jaxpr/all_to_all | solution.py:15
  969.9 50.7 %copy-start.3 = (f32[6,128]{1,0:T(8,128)S(1)}, f32[6,128]{1,0:T(8,128)}, u32[]{:S(2)}) copy-start(f32[6,128]{1,0:T(8,128)} %get-tuple-element.746) | copy-start | bytes 9220 | tf_op jit(solution)/shard_map/while
  1002.2 17.3 %all-to-all-start.1 = ((f32[6,128,8]{0,2,1:T(8,128)}), f32[6,128,8]{0,2,1:T(8,128)S(1)}, u32[]{:S(2)}, u32[]{:S(2)}) async-start(f32[6,128,8]{0,2,1:T(8,128)} %bitcast.107), calls=%async_computation.1 | async-start | bytes 1048576 | tf_op jit(solution)/shard_map/while/body/eval_jaxpr/all_to_all | solution.py:20
  1027.1 18.3 %all-to-all-start = ((f32[6,128,8]{0,2,1:T(8,128)}), f32[6,128,8]{0,2,1:T(8,128)S(1)}, u32[]{:S(2)}, u32[]{:S(2)}) async-start(f32[6,128,8]{0,2,1:T(8,128)} %bitcast.98), calls=%async_computation | async-start | bytes 1048576 | tf_op jit(solution)/shard_map/while/body/eval_jaxpr/all_to_all | solution.py:15
  1061.7 50.7 %copy-start.3 = (f32[6,128]{1,0:T(8,128)S(1)}, f32[6,128]{1,0:T(8,128)}, u32[]{:S(2)}) copy-start(f32[6,128]{1,0:T(8,128)} %get-tuple-element.746) | copy-start | bytes 9220 | tf_op jit(solution)/shard_map/while
  1094.0 17.3 %all-to-all-start.1 = ((f32[6,128,8]{0,2,1:T(8,128)}), f32[6,128,8]{0,2,1:T(8,128)S(1)}, u32[]{:S(2)}, u32[]{:S(2)}) async-start(f32[6,128,8]{0,2,1:T(8,128)} %bitcast.107), calls=%async_computation.1 | async-start | bytes 1048576 | tf_op jit(solution)/shard_map/while/body/eval_jaxpr/all_to_all | solution.py:20
  1118.9 18.3 %all-to-all-start = ((f32[6,128,8]{0,2,1:T(8,128)}), f32[6,128,8]{0,2,1:T(8,128)S(1)}, u32[]{:S(2)}, u32[]{:S(2)}) async-start(f32[6,128,8]{0,2,1:T(8,128)} %bitcast.98), calls=%async_computation | async-start | bytes 1048576 | tf_op jit(solution)/shard_map/while/body/eval_jaxpr/all_to_all | solution.py:15
  1153.5 50.7 %copy-start.3 = (f32[6,128]{1,0:T(8,128)S(1)}, f32[6,128]{1,0:T(8,128)}, u32[]{:S(2)}) copy-start(f32[6,128]{1,0:T(8,128)} %get-tuple-element.746) | copy-start | bytes 9220 | tf_op jit(solution)/shard_map/while
  1185.8 17.3 %all-to-all-start.1 = ((f32[6,128,8]{0,2,1:T(8,128)}), f32[6,128,8]{0,2,1:T(8,128)S(1)}, u32[]{:S(2)}, u32[]{:S(2)}) async-start(f32[6,128,8]{0,2,1:T(8,128)} %bitcast.107), calls=%async_computation.1 | async-start | bytes 1048576 | tf_op jit(solution)/shard_map/while/body/eval_jaxpr/all_to_all | solution.py:20
  1210.7 18.3 %all-to-all-start = ((f32[6,128,8]{0,2,1:T(8,128)}), f32[6,128,8]{0,2,1:T(8,128)S(1)}, u32[]{:S(2)}, u32[]{:S(2)}) async-start(f32[6,128,8]{0,2,1:T(8,128)} %bitcast.98), calls=%async_computation | async-start | bytes 1048576 | tf_op jit(solution)/shard_map/while/body/eval_jaxpr/all_to_all | solution.py:15
  1245.3 50.7 %copy-start.3 = (f32[6,128]{1,0:T(8,128)S(1)}, f32[6,128]{1,0:T(8,128)}, u32[]{:S(2)}) copy-start(f32[6,128]{1,0:T(8,128)} %get-tuple-element.746) | copy-start | bytes 9220 | tf_op jit(solution)/shard_map/while
  1277.6 17.3 %all-to-all-start.1 = ((f32[6,128,8]{0,2,1:T(8,128)}), f32[6,128,8]{0,2,1:T(8,128)S(1)}, u32[]{:S(2)}, u32[]{:S(2)}) async-start(f32[6,128,8]{0,2,1:T(8,128)} %bitcast.107), calls=%async_computation.1 | async-start | bytes 1048576 | tf_op jit(solution)/shard_map/while/body/eval_jaxpr/all_to_all | solution.py:20
  1302.5 18.3 %all-to-all-start = ((f32[6,128,8]{0,2,1:T(8,128)}), f32[6,128,8]{0,2,1:T(8,128)S(1)}, u32[]{:S(2)}, u32[]{:S(2)}) async-start(f32[6,128,8]{0,2,1:T(8,128)} %bitcast.98), calls=%async_computation | async-start | bytes 1048576 | tf_op jit(solution)/shard_map/while/body/eval_jaxpr/all_to_all | solution.py:15
  1337.1 50.7 %copy-start.3 = (f32[6,128]{1,0:T(8,128)S(1)}, f32[6,128]{1,0:T(8,128)}, u32[]{:S(2)}) copy-start(f32[6,128]{1,0:T(8,128)} %get-tuple-element.746) | copy-start | bytes 9220 | tf_op jit(solution)/shard_map/while
  1369.4 17.3 %all-to-all-start.1 = ((f32[6,128,8]{0,2,1:T(8,128)}), f32[6,128,8]{0,2,1:T(8,128)S(1)}, u32[]{:S(2)}, u32[]{:S(2)}) async-start(f32[6,128,8]{0,2,1:T(8,128)} %bitcast.107), calls=%async_computation.1 | async-start | bytes 1048576 | tf_op jit(solution)/shard_map/while/body/eval_jaxpr/all_to_all | solution.py:20
  1394.3 18.3 %all-to-all-start = ((f32[6,128,8]{0,2,1:T(8,128)}), f32[6,128,8]{0,2,1:T(8,128)S(1)}, u32[]{:S(2)}, u32[]{:S(2)}) async-start(f32[6,128,8]{0,2,1:T(8,128)} %bitcast.98), calls=%async_computation | async-start | bytes 1048576 | tf_op jit(solution)/shard_map/while/body/eval_jaxpr/all_to_all | solution.py:15
  1428.9 50.7 %copy-start.3 = (f32[6,128]{1,0:T(8,128)S(1)}, f32[6,128]{1,0:T(8,128)}, u32[]{:S(2)}) copy-start(f32[6,128]{1,0:T(8,128)} %get-tuple-element.746) | copy-start | bytes 9220 | tf_op jit(solution)/shard_map/while
  1461.2 17.3 %all-to-all-start.1 = ((f32[6,128,8]{0,2,1:T(8,128)}), f32[6,128,8]{0,2,1:T(8,128)S(1)}, u32[]{:S(2)}, u32[]{:S(2)}) async-start(f32[6,128,8]{0,2,1:T(8,128)} %bitcast.107), calls=%async_computation.1 | async-start | bytes 1048576 | tf_op jit(solution)/shard_map/while/body/eval_jaxpr/all_to_all | solution.py:20
  (64 other events, 2704.0 us)
where the time goes:
time: 1480 us
  waiting for transfers between devices  438 us (30%)
  blocking collectives  425 us (29%)
  matrix products  263 us (18%)
  starting transfers between devices  138 us (9%)
  local copies, waits for them, and re-layouts  113 us (8%)
  other arithmetic  100 us (7%)
    dot_general x16, matrix products, advance(): jnp.einsum('src,sc->sr', inverses, injection, precision=lax.Precision.HIG...  263 us
    all_gather x16, blocking collectives, advance(): port_currents = lax.all_gather(own_ports, 'line', axis=1, tiled=True)  221 us
    all_to_all x16, waiting for transfers between devices, move_back(): lax.all_to_all(outgoing, ('net', 'line'), split_axis=1, concat_axis=1, ti...  219 us
    all_to_all x16, waiting for transfers between devices, move_forward(): lax.all_to_all(sending, ('net', 'line'), split_axis=1, concat_axis=1, til...  219 us
    all_gather x16, blocking collectives, advance(): gathered = lax.all_gather(solved, 'line', axis=1, tiled=True)  204 us
    all_to_all x16, starting transfers between devices, move_back(): lax.all_to_all(outgoing, ('net', 'line'), split_axis=1, concat_axis=1, ti...  80.7 us
    all_to_all x16, starting transfers between devices, move_forward(): lax.all_to_all(sending, ('net', 'line'), split_axis=1, concat_axis=1, til...  57.3 us
    scatter x16, local copies, waits for them, and re-layouts, advance(): jnp.zeros((mode_count, slot_width), jnp.float32).at[:, port_flat]  30.8 us
  transfers between devices with their start and end apart: 32, of which 32 were waited for; matrix products, arithmetic and copies ran while one was open for 0% of the time, Pallas kernels for 0%

commit v1 on v0

--- a/solution.py
+++ b/solution.py
@@ -1,7 +1,436 @@
+import functools
 import jax
 import jax.numpy as jnp
 from jax import lax
+from jax.experimental import pallas as pl
+from jax.experimental.pallas import tpu as pltpu
 from jax.sharding import PartitionSpec as P
+
+MESH = pl.DeviceIdType.MESH
+VMEM_CAP = 56 * 1024 * 1024
+DEVICES = 128
+SLOTS = 16
+ENDS = 256
+RING = (0, 1, 2, 1)
+OFFSETS = sorted(
+    [(a, b, c, e) for a in range(4) for b in range(4) for c in range(4) for e in range(2) if (a, b, c, e) != (0, 0, 0, 0)],
+    key=lambda o: -(RING[o[0]] + RING[o[1]] + RING[o[2]] + o[3]),
+)
+
+
+def place():
+    i = lax.axis_index("net")
+    z = lax.axis_index("line")
+    return i, z
+
+
+def peer(i, z, offset):
+    dy, dx, dz, dc = offset
+    y, x, zz, c = i // 4, lax.rem(i, 4), z // 2, lax.rem(z, 2)
+    ni = lax.rem(y + dy, 4) * 4 + lax.rem(x + dx, 4)
+    nz = lax.rem(zz + dz, 4) * 2 + lax.rem(c + dc, 2)
+    return ni, nz
+
+
+def greet_all(i, z):
+    barrier = pltpu.get_barrier_semaphore()
+    for offset in OFFSETS:
+        pl.semaphore_signal(barrier, inc=1, device_id=peer(i, z, offset), device_id_type=MESH)
+    pl.semaphore_wait(barrier, len(OFFSETS))
+
+
+def drain(ref, count, sem):
+    part = ref.at[pl.ds(0, count)]
+    pltpu.make_async_copy(part, part, sem).wait()
+
+
+def swap_all_kernel(x_ref, o_ref, send_sem, recv_sem, own_sem):
+    i, z = place()
+    me = i * 8 + z
+    greet_all(i, z)
+    own = pltpu.make_async_copy(x_ref.at[me], o_ref.at[me], own_sem)
+    own.start()
+    for offset in OFFSETS:
+        ni, nz = peer(i, z, offset)
+        pltpu.make_async_remote_copy(
+            src_ref=x_ref.at[ni * 8 + nz], dst_ref=o_ref.at[me], send_sem=send_sem, recv_sem=recv_sem,
+            device_id=(ni, nz), device_id_type=MESH,
+        ).start()
+    own.wait()
+    drain(o_ref, DEVICES - 1, recv_sem)
+    drain(x_ref, DEVICES - 1, send_sem)
+
+
+def swap_line_kernel(x_ref, o_ref, send_sem, recv_sem, own_sem):
+    i, z = place()
+    barrier = pltpu.get_barrier_semaphore()
+    for k in range(1, 8):
+        pl.semaphore_signal(barrier, inc=1, device_id=(i, lax.rem(z + k, 8)), device_id_type=MESH)
+    pl.semaphore_wait(barrier, 7)
+    own = pltpu.make_async_copy(x_ref.at[z], o_ref.at[z], own_sem)
+    own.start()
+    for k in range(1, 8):
+        nz = lax.rem(z + k, 8)
+        pltpu.make_async_remote_copy(
+            src_ref=x_ref.at[nz], dst_ref=o_ref.at[z], send_sem=send_sem, recv_sem=recv_sem,
+            device_id=(i, nz), device_id_type=MESH,
+        ).start()
+    own.wait()
+    drain(o_ref, 7, recv_sem)
+    drain(x_ref, 7, send_sem)
+
+
+def swap(kernel, x, collective_id, name):
+    return pl.pallas_call(
+        kernel,
+        out_shape=jax.ShapeDtypeStruct(x.shape, x.dtype),
+        in_specs=[pl.BlockSpec(memory_space=pl.ANY)],
+        out_specs=pl.BlockSpec(memory_space=pl.ANY),
+        scratch_shapes=[pltpu.SemaphoreType.DMA] * 3,
+        compiler_params=pltpu.CompilerParams(collective_id=collective_id, has_side_effects=True),
+        name=name,
+    )(x)
+
+
+def response_kernel(
+    yd, yr, ydir, ys_in, pd, pr, ps_in, delay, waves, hist0, zero_in, ht, g, yst, pst, yim, pim, hbuf
+):
+    steps = hist0.shape[1]
+    yst[...] = ys_in[...]
+    pst[...] = ps_in[...]
+    yim[...] = yr[...]
+    pim[...] = pr[...]
+    depth = lax.broadcasted_iota(jnp.int32, (6, 64, 128), 1)
+
+    def step(n, carry):
+        pick = depth == (64 + n - delay[...])[:, None, :]
+        ydec, pdec, pres = yd[...], pd[...], pr[...]
+        for e in range(2):
+            seen = jnp.sum(jnp.where(pick, waves[1 - e], 0.0), axis=1)
+            now = pdec * pst[e] + pres * seen[:, None, :]
+            pst[e] = now
+            hist0[e, n] = jnp.sum(now, axis=1)
+            free = ydec * yst[e]
+            yst[e] = free
+            zero_in[e, n] = jnp.sum(free, axis=1)
+        first = jnp.where(n == 0, 1.0, 0.0)
+        pnow, ynow = pim[...], yim[...]
+        hbuf[n] = jnp.sum(pnow, axis=1)
+        g[n] = jnp.sum(ynow, axis=1) + first * ydir[...]
+        pim[...] = pnow * pdec
+        yim[...] = ynow * ydec
+        return carry
+
+    lax.fori_loop(0, steps, step, 0)
+    lag = delay[...]
+    ht[0] = jnp.zeros((6, 128), jnp.float32)
+    for k in range(1, steps):
+        total = jnp.zeros((6, 128), jnp.float32)
+        for m in range(k):
+            total = total + jnp.where(lag == k - m, hbuf[m], 0.0)
+        ht[k] = total
+
+
+def line_responses(yc_decay, yc_residue, yc_direct, yc_state, prop_decay, prop_residue, prop_state, delay_steps, wave_buffer):
+    two = jax.ShapeDtypeStruct((2, 16, 6, 128), jnp.float32)
+    one = jax.ShapeDtypeStruct((16, 6, 128), jnp.float32)
+    vm = pl.BlockSpec(memory_space=pltpu.VMEM)
+    return pl.pallas_call(
+        response_kernel,
+        out_shape=(two, two, one, one),
+        in_specs=[vm] * 9,
+        out_specs=(vm,) * 4,
+        scratch_shapes=[
+            pltpu.VMEM((2, 6, 30, 128), jnp.float32),
+            pltpu.VMEM((2, 6, 30, 128), jnp.float32),
+            pltpu.VMEM((6, 30, 128), jnp.float32),
+            pltpu.VMEM((6, 30, 128), jnp.float32),
+            pltpu.VMEM((16, 6, 128), jnp.float32),
+        ],
+        compiler_params=pltpu.CompilerParams(vmem_limit_bytes=VMEM_CAP),
+        name="line_responses",
+    )(yc_decay, yc_residue, yc_direct, yc_state, prop_decay, prop_residue, prop_state, delay_steps, wave_buffer)
+
+
+def split(value):
+    high = value.astype(jnp.bfloat16)
+    low = (value - high.astype(jnp.float32)).astype(jnp.bfloat16)
+    return high, low
+
+
+def steps_kernel(
+    inverses, v0_send, hist_in, zero_in, ht, g, mmap, send_rank, send_dev, recv_rank, recv_dev, over_in,
+    inject_out, current_out, flag_out,
+    block, v0, solve, hacc, cacc, to_row, from_row, send_buf, recv_buf,
+    block_send, block_recv, v0_sendsem, v0_recv, own_sem, wave_send, wave_recv,
+):
+    i, z = place()
+    me = i * 8 + z
+    steps = 16
+    lane = lax.broadcasted_iota(jnp.int32, (1, 128), 1)
+    greet_all(i, z)
+
+    def block_copy(src_z, dst_z):
+        return inverses.at[pl.ds(dst_z * 4, 4), :, pl.ds(0, 384)], block.at[src_z]
+
+    @pl.when(z < 3)
+    def _send():
+        for k in range(1, 8):
+            nz = lax.rem(z + k, 8)
+            pltpu.make_async_remote_copy(
+                src_ref=v0_send.at[nz], dst_ref=v0.at[z], send_sem=v0_sendsem, recv_sem=v0_recv.at[z],
+                device_id=(i, nz), device_id_type=MESH,
+            ).start()
+        for k in range(1, 8):
+            nz = lax.rem(z + k, 8)
+            src, dst = block_copy(z, nz)
+            pltpu.make_async_remote_copy(
+                src_ref=src, dst_ref=dst, send_sem=block_send, recv_sem=block_recv.at[z],
+                device_id=(i, nz), device_id_type=MESH,
+            ).start()
+        src, dst = block_copy(z, z)
+        own = pltpu.make_async_copy(src, dst, own_sem.at[0])
+        own.start()
+        own2 = pltpu.make_async_copy(v0_send.at[z], v0.at[z], own_sem.at[1])
+        own2.start()
+        own.wait()
+        own2.wait()
+
+    hacc[...] = jnp.zeros(hacc.shape, jnp.float32)
+    cacc[...] = jnp.zeros(cacc.shape, jnp.float32)
+    hacc[0:steps] = hist_in[...]
+    cacc[0:steps] = zero_in[...]
+    to_row[...] = jnp.where(
+        lax.broadcasted_iota(jnp.int32, (DEVICES, ENDS), 0) == send_dev[...], 1.0, 0.0
+    ).astype(jnp.bfloat16)
+    from_row[...] = jnp.where(
+        lax.broadcasted_iota(jnp.int32, (ENDS, DEVICES), 1) == recv_dev[...], 1.0, 0.0
+    ).astype(jnp.bfloat16)
+    mode_pick = jnp.where(
+        lax.rem(lax.broadcasted_iota(jnp.int32, (8, 256), 1), 128) // SLOTS
+        == lax.broadcasted_iota(jnp.int32, (8, 256), 0), 1.0, 0.0
+    ).astype(jnp.bfloat16)
+
+    for src_z in range(3):
+        @pl.when(z != src_z)
+        def _wait():
+            pltpu.make_async_copy(block.at[src_z], block.at[src_z], block_recv.at[src_z]).wait()
+            pltpu.make_async_copy(v0.at[src_z], v0.at[src_z], v0_recv.at[src_z]).wait()
+
+    def build(t, carry):
+        for src_z in range(3):
+            for h in range(2):
+                for kk in range(2):
+                    rows = block[src_z, t * 2 + h, kk * 64:(kk + 1) * 64, :]
+                    row0 = (src_z * 2 + kk) * 128 + h * 64
+                    for k in range(6):
+                        tile = rows[:, (k // 2) * 128:(k // 2 + 1) * 128]
+                        if k % 2 != h:
+                            tile = pltpu.roll(tile, 64, 1)
+                        tile = jnp.where((lane // 64) == h, tile, 0.0)
+                        high, low = split(tile)
+                        solve[t, row0:row0 + 64, k * 128:(k + 1) * 128] = high
+                        solve[t, 768 + row0:768 + row0 + 64, k * 128:(k + 1) * 128] = low
+        return carry
+
+    lax.fori_loop(0, 2, build, 0)
+
+    over = over_in[0:1, 0:1]
+    flag_lane = jnp.where(lane == 127, 1.0, 0.0) * over
+
+    def step(n, carry):
+        delayed, worst = carry
+        par = lax.rem(n, 2)
+        hist = hacc[n] + ht[1] * delayed
+        phase = [jnp.sum(mmap[k] * hist, axis=0, keepdims=True) for k in range(6)]
+        volts = []
+        for t in range(2):
+            inj = jnp.concatenate([p[:, t * 128:(t + 1) * 128] for p in phase], axis=1)
+            inject_out[t, pl.ds(n, 1), :] = inj
+            high, low = split(inj)
+            left = jnp.concatenate([high, low], axis=0)
+            both = lax.dot_general(
+                left, solve[t], (((1,), (1,)), ((), ())), preferred_element_type=jnp.float32
+            )
+            total = jnp.sum(both, axis=0, keepdims=True)
+            total = total[:, :768] + total[:, 768:]
+            base = jnp.concatenate([v0[a, t, pl.ds(n, 1), :] for a in range(3)], axis=1)
+            volts.append(total + base)
+        modal = jnp.zeros((8, ENDS), jnp.float32)
+        for k in range(6):
+            row = jnp.concatenate([v[:, k * 128:(k + 1) * 128] for v in volts], axis=1)
+            modal = modal + mmap[k] * row
+        charac = cacc[n] + g[0] * modal
+        wave = 2.0 * charac - hist
+        current_out[n] = charac - hist
+
+        @pl.when(n < steps - 1)
+        def _exchange():
+            @pl.when(n > 1)
+            def _free():
+                drain(send_buf.at[par], DEVICES - 1, wave_send.at[par])
+            spread = jnp.concatenate(
+                [jnp.broadcast_to(wave[j:j + 1], (SLOTS, ENDS)) for j in range(8)], axis=0
+            )
+            slot = lax.rem(lax.broadcasted_iota(jnp.int32, (DEVICES, ENDS), 0), SLOTS)
+            spread = jnp.where(slot == send_rank[...], spread, 0.0)
+            high, low = split(spread)
+            rows = lax.dot_general(
+                to_row[...], jnp.concatenate([high, low], axis=0), (((1,), (1,)), ((), ())),
+                preferred_element_type=jnp.float32,
+            )
+            send_buf[par] = (rows[:, :128] + rows[:, 128:] + flag_lane)[:, None, :]
+            for offset in OFFSETS:
+                ni, nz = peer(i, z, offset)
+                pltpu.make_async_remote_copy(
+                    src_ref=send_buf.at[par, ni * 8 + nz], dst_ref=recv_buf.at[par, me],
+                    send_sem=wave_send.at[par], recv_sem=wave_recv.at[par],
+                    device_id=(ni, nz), device_id_type=MESH,
+                ).start()
+            recv_buf[par, me] = send_buf[par, me]
+
+        for k in range(2, steps):
+            hacc[n + k - 1] = hacc[n + k - 1] + ht[k] * delayed
+        for k in range(1, steps):
+            cacc[n + k] = cacc[n + k] + g[k] * modal
+
+        @pl.when(n < steps - 1)
+        def _arrive():
+            drain(recv_buf.at[par], DEVICES - 1, wave_recv.at[par])
+
+        got = recv_buf[par].reshape(DEVICES, 128)
+        worst = jnp.maximum(worst, jnp.max(got[:, 127:128], axis=0, keepdims=True))
+        high, low = split(got)
+        mine = jnp.dot(from_row[...], jnp.concatenate([high, low], axis=1), preferred_element_type=jnp.float32)
+        slot = lax.rem(lax.broadcasted_iota(jnp.int32, (ENDS, 256), 1), SLOTS)
+        mine = jnp.where(slot == recv_rank[...], mine, 0.0).astype(jnp.bfloat16)
+        delayed = lax.dot_general(mode_pick, mine, (((1,), (1,)), ((), ())), preferred_element_type=jnp.float32)
+        return delayed, worst
+
+    delayed, worst = lax.fori_loop(
+        0, steps, step, (jnp.zeros((8, ENDS), jnp.float32), jnp.zeros((1, 1), jnp.float32))
+    )
+    flag_out[...] = jnp.broadcast_to(worst, flag_out.shape)
+    drain(send_buf.at[0], DEVICES - 1, wave_send.at[0])
+    drain(send_buf.at[1], DEVICES - 1, wave_send.at[1])
+
+    @pl.when(z < 3)
+    def _sent():
+        pltpu.make_async_copy(v0_send.at[pl.ds(0, 7)], v0_send.at[pl.ds(0, 7)], v0_sendsem).wait()
+        seven = inverses.at[pl.ds(0, 28), :, pl.ds(0, 384)]
+        pltpu.make_async_copy(seven, seven, block_send).wait()
+
+
+def run_steps(inverses, v0_send, hist, zero_in, ht, g, mmap, send_rank, send_dev, recv_rank, recv_dev, over):
+    vm = pl.BlockSpec(memory_space=pltpu.VMEM)
+    any_ = pl.BlockSpec(memory_space=pl.ANY)
+    f32 = jnp.float32
+    dma = pltpu.SemaphoreType.DMA
+    return pl.pallas_call(
+        steps_kernel,
+        out_shape=(
+            jax.ShapeDtypeStruct((2, 16, 768), f32),
+            jax.ShapeDtypeStruct((16, 8, ENDS), f32),
+            jax.ShapeDtypeStruct((8, 128), f32),
+        ),
+        in_specs=[any_, any_] + [vm] * 10,
+        out_specs=(vm, vm, vm),
+        scratch_shapes=[
+            pltpu.VMEM((3, 4, 128, 384), f32),
+            pltpu.VMEM((3, 2, 16, 256), f32),
+            pltpu.VMEM((2, 1536, 768), jnp.bfloat16),
+            pltpu.VMEM((32, 8, ENDS), f32),
+            pltpu.VMEM((32, 8, ENDS), f32),
+            pltpu.VMEM((DEVICES, ENDS), jnp.bfloat16),
+            pltpu.VMEM((ENDS, DEVICES), jnp.bfloat16),
+            pltpu.VMEM((2, DEVICES, 1, 128), f32),
+            pltpu.VMEM((2, DEVICES, 1, 128), f32),
+            dma, dma((3,)), dma, dma((3,)), dma((2,)), dma((2,)), dma((2,)),
+        ],
+        compiler_params=pltpu.CompilerParams(collective_id=9, has_side_effects=True, vmem_limit_bytes=VMEM_CAP),
+        name="transient_steps",
+    )(inverses, v0_send, hist, zero_in, ht, g, mmap, send_rank, send_dev, recv_rank, recv_dev, over)
+
+
+def body(
+    inverses, node_counts, sources, port_slot, end_slot, modal_map, delay_steps, wave_buffer, yc_decay, yc_residue,
+    yc_direct, yc_state, prop_decay, prop_residue, prop_state,
+):
+    i, z = place()
+    f32 = jnp.float32
+    port_flat = port_slot.reshape(-1)
+    end_flat = end_slot.reshape(-1)
+
+    sub = jnp.arange(32, dtype=jnp.int32)[:, None]
+    port = z * 8 + jnp.arange(8, dtype=jnp.int32)[None, :]
+    code = ((i * 8 + sub // 4) * ENDS + (sub % 4) * 64 + port).astype(f32).reshape(-1)
+    codes = jnp.zeros((1024,), f32).at[port_flat].set(code)
+    codes = jnp.pad(codes.reshape(DEVICES, 1, 8), ((0, 0), (0, 0), (0, 120)))
+    codes = swap(swap_all_kernel, codes, 1, "owner_codes")
+    end_code = codes[:, 0, :8].reshape(-1)[end_flat].reshape(2, 128)
+
+    hist0, zero_in, ht, g = line_responses(
+        yc_decay, yc_residue, yc_direct, yc_state, prop_decay, prop_residue, prop_state, delay_steps, wave_buffer
+    )
+    shared = jnp.concatenate([ht.reshape(96, 128), g.reshape(96, 128), modal_map.reshape(36, 128)], axis=0)
+    table = jnp.concatenate(
+        [
+            hist0.reshape(2, 96, 128), zero_in.reshape(2, 96, 128),
+            jnp.broadcast_to(shared[None], (2, 228, 128)), end_code[::-1][:, None, :],
+            jnp.zeros((2, 512 - 421, 128), f32),
+        ],
+        axis=1,
+    )
+    table = table.transpose(0, 2, 1).reshape(ENDS, 512)
+    holder = jnp.zeros((1024,), jnp.int32).at[end_flat].set(jnp.arange(ENDS, dtype=jnp.int32))
+    moved = swap(swap_all_kernel, table[holder].reshape(DEVICES, 8, 512), 2, "tables_to_ports")
+    at_ports = moved.reshape(1024, 512)[port_flat].reshape(8, 32, 512)
+    at_owner = swap(swap_line_kernel, at_ports, 3, "tables_to_owners")
+    mine = at_owner.reshape(8, 4, 8, 512).transpose(3, 1, 0, 2).reshape(512, ENDS)
+
+    def padded(part):
+        return jnp.pad(part.reshape(-1, 6, ENDS), ((0, 0), (0, 2), (0, 0)))
+
+    hist_t, zero_t, ht_t, g_t, map_t = (
+        padded(mine[0:96]), padded(mine[96:192]), padded(mine[192:288]), padded(mine[288:384]), padded(mine[384:420])
+    )
+    partner = mine[420].astype(jnp.int32)
+    dev, pos = partner // ENDS, partner % ENDS
+    same = dev[:, None] == dev[None, :]
+    own = jnp.arange(ENDS, dtype=jnp.int32)
+    send_rank = jnp.sum((same & (own[:, None] < own[None, :])).astype(jnp.int32), axis=0)
+    recv_rank = jnp.sum((same & (pos[:, None] < pos[None, :])).astype(jnp.int32), axis=0)
+    over = jnp.full((8, 128), jnp.max(send_rank) >= SLOTS).astype(f32)
+
+    still = jnp.einsum("src,nsc->nsr", inverses, sources, precision=lax.Precision.HIGH)
+    v0_send = still.reshape(16, 8, 2, 2, 2, 64).transpose(1, 2, 0, 4, 3, 5).reshape(8, 2, 16, 256)
+
+    inject, current, flag = run_steps(
+        inverses, v0_send, hist_t, zero_t, ht_t, g_t, map_t, send_rank[None, :], dev[None, :], recv_rank[:, None],
+        dev[:, None], over,
+    )
+
+    def quick(_):
+        ports = lax.all_gather(inject, "line", axis=0)
+        ports = ports.reshape(8, 2, 16, 6, 2, 64).transpose(2, 0, 1, 4, 3, 5).reshape(16, 32, 384)
+        volts = still + jnp.einsum("src,nsc->nsr", inverses[:, :, :384], ports, precision=lax.Precision.HIGH)
+        row_ids = z * 128 + jnp.arange(128, dtype=jnp.int32)
+        volts = jnp.where((row_ids[None, :] < node_counts[:, None])[None], volts, 0.0)
+        back = current[:, :6].reshape(96, 4, 8, 8).transpose(2, 1, 3, 0).reshape(8, 32, 96)
+        back = swap(swap_line_kernel, jnp.pad(back, ((0, 0), (0, 0), (0, 32))), 4, "currents_to_ports")
+        source_port = jnp.zeros((1024,), jnp.int32).at[port_flat].set(jnp.arange(ENDS, dtype=jnp.int32))
+        back = back.reshape(ENDS, 128)[source_port].reshape(DEVICES, 8, 128)
+        back = swap(swap_all_kernel, back, 5, "currents_to_lines")
+        lines = back.reshape(1024, 128)[end_flat][:, :96].reshape(2, 128, 16, 6)
+        return volts, lines.transpose(2, 0, 3, 1)
+
+    def general(_):
+        return general_body(
+            inverses, node_counts, sources, port_slot, end_slot, modal_map, delay_steps, wave_buffer, yc_decay,
+            yc_residue, yc_direct, yc_state, prop_decay, prop_residue, prop_state,
+        )
+
+    return lax.cond(flag[0, 0] > 0.0, general, quick, 0)
 
 
 def read_delayed(extended, delay_steps, step_index, buffer_len):
@@ -21,7 +450,7 @@
     return arrived
 
 
-def body(
+def general_body(
     inverses,
     node_counts,
     sources,

time: 1480 us -> 403 us (0.27)
  waiting for transfers between devices: 438 us -> 0 us
  blocking collectives: 425 us -> 14.3 us
  Pallas kernels: 0 us -> 281 us
  matrix products: 263 us -> 26.9 us
  starting transfers between devices: 138 us -> 0 us
  other arithmetic: 100 us -> 3.22 us
  local copies, waits for them, and re-layouts: 113 us -> 69.1 us
    all_to_all x32 -> x0, waiting for transfers between devices: 438 us -> none  [the longest x16 219 us: move_back(): lax.all_to_all(outgoing, ('net', 'line'), split_axis=1, concat_axis=1, ti...]
    all_gather x32 -> x1, blocking collectives: 425 us -> 14.3 us  [quick(): ports = lax.all_gather(inject, 'line', axis=0)]
    pallas_call x0 -> x7, Pallas kernels: none -> 281 us  [the longest x1 201 us: run_steps(): pl.pallas_call(steps_kernel, out_shape=(jax.ShapeDtypeStruct((2, 16, 768)...]
    dot_general x16 -> x2, matrix products: 263 us -> 26.9 us  [the longest x1 21.4 us: body(): jnp.einsum('src,nsc->nsr', inverses, sources, precision=lax.Precision.HIGH)]
    all_to_all x32 -> x0, starting transfers between devices: 138 us -> none  [the longest x16 80.7 us: move_back(): lax.all_to_all(outgoing, ('net', 'line'), split_axis=1, concat_axis=1, ti...]
    scatter x32 -> x3, local copies, waits for them, and re-layouts: 61.5 us -> 4.59 us  [the longest x1 1.78 us: body(): jnp.zeros((1024,), jnp.int32).at[end_flat]]
    reduce_sum x80 -> x1, other arithmetic: 41.7 us -> 0.15 us  [body(): jnp.sum((same & (pos[:, None] < pos[None, :])).astype(jnp.int32), axis=0)]
    dynamic_update_slice x48 -> x0, other arithmetic: 21.1 us -> none  [the longest x16 11.1 us: advance(): lax.dynamic_update_slice_in_dim(volts_acc, solved[None], step_index, 0)]
  transfers between devices with their start and end apart: 32 -> 0, of which waited for: 32 -> 0; matrix products, arithmetic and copies ran while one was open for 0% -> 0% of each run, Pallas kernels for 0% -> 0%
where the time goes in v1:
time: 403 us; the launch traced here: 398 us
  Pallas kernels  281 us (70%)
  local copies, waits for them, and re-layouts  69.1 us (17%)
  matrix products  26.9 us (7%)
  blocking collectives  14.3 us (4%)
    pallas_call x1, Pallas kernels, run_steps(): pl.pallas_call(steps_kernel, out_shape=(jax.ShapeDtypeStruct((2, 16, 768)...  201 us
    pallas_call x5, Pallas kernels, swap(): pl.pallas_call(kernel, out_shape=jax.ShapeDtypeStruct(x.shape, x.dtype),...  75.8 us
    dot_general x1, matrix products, body(): jnp.einsum('src,nsc->nsr', inverses, sources, precision=lax.Precision.HIGH)  21.4 us
    all_gather x1, blocking collectives, quick(): ports = lax.all_gather(inject, 'line', axis=0)  14.3 us
    reshape x1, local copies, waits for them, and re-layouts, body(): at_owner.reshape(8, 4, 8, 512).transpose(3, 1, 0, 2).reshape(512, ENDS)  8.22 us

profile of v1, /device:TPU:1, one launch (start us, length us, event | category | flops | bytes accessed | tf_op | source)
XLA Modules:
  0.0 398.2 jit_solution(16129515883281381233)
XLA Ops:
  0.7 1.6 copy.235.ys_in
  2.3 1.6 copy.236.ps_in
  3.9 4.6 %line_responses.1 = (f32[2,16,6,128]{3,2,1,0:T(8,128)}, f32[2,16,6,128]{3,2,1,0:T(8,128)}, f32[16,6,128]{2,1,0:T(8,128)}, f32[16,6,128]{2,1,0:T(8,128)}) custom-call(f32[6,30,128]{2,1,0:T(8,128)} %yd.1, f32[6,30,128]{2,1,0:T(8,128)} %yr.1, f32[6,128]{1,0:T(8,128)} %ydir.1, f32[2,6,30,128]{3,2,1,0:T(8,128)} %copy.235.ys_in, f32[6,30,128]{2,1,0:T(8,128)} %pd.1, ...), custom_call_target="tpu_custom_call" | custom-call | tf_op jit(solution)/shard_map/line_responses/pallas_call | solution.py:138
  8.5 0.9 reshape.624
  9.4 0.8 reshape.625
  10.9 1.4 scatter_custom_fusion.3
  12.4 0.7 pad.37.x_ref
  13.1 15.1 %owner_codes.1 = f32[128,1,128]{2,1,0:T(1,128)} custom-call(f32[128,1,128]{2,1,0:T(1,128)} %pad.37.x_ref), custom_call_target="tpu_custom_call" | custom-call | tf_op jit(solution)/shard_map/owner_codes/pallas_call | solution.py:84
  28.2 1.0 slice_reduce_fusion
  29.6 1.4 gather_fusion.4
  31.9 1.8 scatter_custom_fusion.4
  33.7 4.9 %gather_fusion.5 = f32[1024,512]{1,0:T(8,128)} fusion(f32[256,512]{1,0:T(8,128)S(1)} %bitcast.171, s32[1024]{0:T(1024)S(1)} %fusion.34), kind=kCustom, calls=%fused_computation.5 | custom fusion | bytes 4198400 | tf_op jit(solution)/shard_map/gather | solution.py:386
  38.6 31.1 %tables_to_ports.1 = f32[128,8,512]{2,1,0:T(8,128)} custom-call(f32[128,8,512]{2,1,0:T(8,128)} %bitcast.180), custom_call_target="tpu_custom_call" | custom-call | tf_op jit(solution)/shard_map/tables_to_ports/pallas_call | solution.py:84
  69.7 3.6 gather_fusion.6
  73.3 10.6 %tables_to_owners.1 = f32[8,32,512]{2,1,0:T(8,128)} custom-call(f32[8,32,512]{2,1,0:T(8,128)} %bitcast.191), custom_call_target="tpu_custom_call" | custom-call | tf_op jit(solution)/shard_map/tables_to_owners/pallas_call | solution.py:84
  84.0 8.2 %copy.251 = f32[8,4,8,512]{2,0,1,3:T(8,128)} copy(f32[8,4,8,512]{3,2,1,0:T(8,128)} %bitcast.192) | data formatting | bytes 1048576 | tf_op jit(solution)/shard_map/reshape | solution.py:389
  92.2 0.7 slice_convert_fusion
  95.1 0.8 copy.256.recv_rank
  95.8 5.3 %fusion.45 = (f32[96,4,8,8]{3,2,1,0:T(8,128)S(1)}, f32[96,4,8,8]{3,2,1,0:T(8,128)S(1)}, f32[96,4,8,8]{3,2,1,0:T(8,128)}, f32[96,4,8,8]{3,2,1,0:T(8,128)}) fusion(f32[512,4,8,8]{3,2,1,0:T(8,128)} %bitcast.174), kind=kLoop, calls=%fused_computation.114 | loop fusion | bytes 786432 | tf_op jit(solution)/shard_map/slice | solution.py:395
  101.1 2.3 reshape.636
  104.1 2.3 reshape.637
  106.3 0.7 pad.39.zero_in
  107.0 0.8 reshape.638
  107.8 0.7 pad.40.ht
  108.5 0.8 reshape.639
  109.3 0.7 pad.41.g
  110.1 0.7 add_select_fusion.recv_dev
  111.4 1.1 slice.78
  113.5 21.4 %fusion.27 = f32[16,32,128]{2,0,1:T(8,128)S(1)} fusion(f32[32,128,1024]{2,1,0:T(8,128)} %inverses.1, f32[16,32,1024]{2,1,0:T(8,128)S(1)} %copy-done), kind=kOutput, calls=%fused_computation.61 | convolution fusion | flops 402653184 | bytes 19136512 | tf_op jit(solution)/shard_map/src,nsc->nsr/dot_general | solution.py:405
  134.9 1.1 reshape.620
  136.0 1.4 copy.290
  137.5 1.2 reshape.621.v0_send
  138.7 200.7 %transient_steps.1 = (f32[2,16,768]{2,1,0:T(8,128)S(1)}, f32[16,8,256]{2,1,0:T(8,128)}, f32[8,128]{1,0:T(8,128)}) custom-call(f32[32,128,1024]{2,1,0:T(8,128)} %inverses.1, f32[8,2,16,256]{3,2,1,0:T(8,128)} %reshape.621.v0_send, f32[16,8,256]{2,1,0:T(8,128)} %pad.38.hist_in, f32[16,8,256]{2,1,0:T(8,128)} %pad.39.zero_in, f32[16,8,256]{2,1,0:T(8,128)} %pad.40.ht, ...), custom_call_target="tpu_custom_call" | custom-call | tf_op jit(solution)/shard_map/transient_steps/pallas_call | solution.py:329
  339.4 1.2 slice.56
  341.3 55.8 %conditional.1 = (f32[16,2,6,128]{3,1,2,0:T(2,128)}, f32[16,32,128]{2,1,0:T(8,128)}) conditional(s32[]{:T(128)} %bitcast.29, (s32[]{:T(128)}, s32[32]{0:T(128)}, f32[2,16,768]{2,1,0:T(8,128)S(1)}, f32[32,128,1024]{2,1,0:T(8,128)}, f32[16,32,128]{2,0,1:T(8,128)S(1)}, /*index=5*/f32[16,8,256]{2,1,0:T(8,128)}, s32[32,8]{0,1:T(8,128)S(1)}, ...), branch_computations={%region_5.7_spmd, %region_7.17_spmd} | conditional | flops 151136896 | bytes 33724768 | solution.py:433
  341.3 14.3 %all-gather = f32[16,16,768]{2,1,0:T(8,128)S(1)} all-gather(f32[2,16,768]{2,1,0:T(8,128)S(1)} %get-tuple-element.475), channel_id=2, replica_groups=mesh['net'=16,'line'=8] {'line'}, dimensions={0}, use_global_device_ids=true | all-gather | bytes 884736 | tf_op jit(solution)/shard_map/cond/branch_0_fun/all_gather | solution.py:414
  355.6 2.2 reshape.578
  357.8 1.7 copy.288
  360.2 5.5 %fusion.10 = f32[16,32,128]{2,0,1:T(8,128)S(1)} fusion(f32[16,32,128]{2,0,1:T(8,128)S(1)} %get-tuple-element.474, f32[32,128,1024]{2,1,0:T(8,128)} %get-tuple-element.476, f32[16,32,384]{2,1,0:T(8,128)S(1)} %reshape.579, pred[32,128]{1,0:T(8,128)(4,1)S(1)} %broadcast_compare_fusion), kind=kOutput, calls=%fused_computation.18 | convolution fusion | flops 151126016 | bytes 7606272 | tf_op jit(solution)/shard_map/cond/branch_0_fun/src,nsc->nsr/dot_general | solution.py:416
  365.8 0.8 copy.266
  366.6 0.9 reshape.580
  367.4 0.9 copy.216
  369.0 5.9 %currents_to_ports.1 = f32[8,32,128]{2,1,0:T(8,128)} custom-call(f32[8,32,128]{2,1,0:T(8,128)} %pad.29.x_ref), custom_call_target="tpu_custom_call" | custom-call | tf_op jit(solution)/shard_map/cond/branch_0_fun/currents_to_ports/pallas_call | solution.py:84
  375.1 1.4 scatter_custom_fusion
  376.5 4.9 %gather_fusion = f32[1024,128]{1,0:T(8,128)} fusion(f32[256,128]{1,0:T(8,128)} %bitcast.172, s32[1024]{0:T(1024)S(1)} %fusion.14), kind=kCustom, calls=%fused_computation | custom fusion | bytes 1052672 | tf_op jit(solution)/shard_map/cond/branch_0_fun/gather | solution.py:422
  381.4 13.1 %currents_to_lines.1 = f32[128,8,128]{2,1,0:T(8,128)} custom-call(f32[128,8,128]{2,1,0:T(8,128)} %bitcast.194), custom_call_target="tpu_custom_call" | custom-call | tf_op jit(solution)/shard_map/cond/branch_0_fun/currents_to_lines/pallas_call | solution.py:84
  394.6 1.8 gather_fusion.1
  396.4 0.7 reshape.587
  (84 shorter events, 7.4 us)
Async XLA Ops:
  0.6 9.6 %copy-start.6 = (f32[6,6,128]{2,1,0:T(8,128)S(1)}, f32[6,6,128]{2,1,0:T(8,128)}, u32[]{:S(2)}) copy-start(f32[6,6,128]{2,1,0:T(8,128)} %param.24) | copy-start | bytes 55300
  0.6 10.0 %copy-start.15 = (s32[32,8]{0,1:T(8,128)S(1)}, s32[32,8]{0,1:T(8,128)}, u32[]{:S(2)}) copy-start(s32[32,8]{0,1:T(8,128)} %param.22) | copy-start | bytes 3076
  0.7 28.7 %copy-start.14 = (s32[2,128]{1,0:T(2,128)S(1)}, s32[2,128]{1,0:T(2,128)}, u32[]{:S(2)}) copy-start(s32[2,128]{1,0:T(2,128)} %param.23) | copy-start | bytes 3076
  8.5 22.7 %copy-start.12 = (f32[2,16,6,128]{3,2,1,0:T(8,128)S(1)}, f32[2,16,6,128]{3,2,1,0:T(8,128)}, u32[]{:S(2)}) copy-start(f32[2,16,6,128]{3,2,1,0:T(8,128)} %get-tuple-element.526) | copy-start | bytes 294916
  8.5 22.9 %copy-start.11 = (f32[2,16,6,128]{3,2,1,0:T(8,128)S(1)}, f32[2,16,6,128]{3,2,1,0:T(8,128)}, u32[]{:S(2)}) copy-start(f32[2,16,6,128]{3,2,1,0:T(8,128)} %get-tuple-element.527) | copy-start | bytes 294916
  93.2 8.0 %copy-start.18 = (s32[256]{0:T(256)}, s32[256]{0:T(256)S(1)}, u32[]{:S(2)}) copy-start(s32[256]{0:T(256)S(1)} %get-tuple-element.735) | copy-start | bytes 3076
  109.3 4.2 %copy-start = (f32[16,32,1024]{2,1,0:T(8,128)S(1)}, f32[16,32,1024]{2,1,0:T(8,128)}, u32[]{:S(2)}) copy-start(f32[16,32,1024]{2,1,0:T(8,128)} %param.21) | copy-start | bytes 6291460
  138.6 202.6 %copy-start.2 = (f32[6,30,128]{2,1,0:T(8,128)S(1)}, f32[6,30,128]{2,1,0:T(8,128)}, u32[]{:S(2)}) copy-start(f32[6,30,128]{2,1,0:T(8,128)} %yd.1) | copy-start | bytes 276484
  138.6 202.6 %copy-start.3 = (f32[6,30,128]{2,1,0:T(8,128)S(1)}, f32[6,30,128]{2,1,0:T(8,128)}, u32[]{:S(2)}) copy-start(f32[6,30,128]{2,1,0:T(8,128)} %yr.1) | copy-start | bytes 276484
  138.6 202.6 %copy-start.4 = (f32[6,30,128]{2,1,0:T(8,128)S(1)}, f32[6,30,128]{2,1,0:T(8,128)}, u32[]{:S(2)}) copy-start(f32[6,30,128]{2,1,0:T(8,128)} %pd.1) | copy-start | bytes 276484
  138.7 202.6 %copy-start.5 = (f32[6,30,128]{2,1,0:T(8,128)S(1)}, f32[6,30,128]{2,1,0:T(8,128)}, u32[]{:S(2)}) copy-start(f32[6,30,128]{2,1,0:T(8,128)} %pr.1) | copy-start | bytes 276484
  138.7 202.6 %copy-start.7 = (f32[2,6,30,128]{3,0,2,1:T(2,128)S(1)}, f32[2,6,30,128]{3,0,2,1:T(2,128)}, u32[]{:S(2)}) copy-start(f32[2,6,30,128]{3,0,2,1:T(2,128)} %param.30) | copy-start | bytes 552964
  138.7 202.6 %copy-start.8 = (f32[2,6,30,128]{3,0,2,1:T(2,128)S(1)}, f32[2,6,30,128]{3,0,2,1:T(2,128)}, u32[]{:S(2)}) copy-start(f32[2,6,30,128]{3,0,2,1:T(2,128)} %param.33) | copy-start | bytes 552964
  138.7 202.6 %copy-start.9 = (s32[6,128]{1,0:T(8,128)S(1)}, s32[6,128]{1,0:T(8,128)}, u32[]{:S(2)}) copy-start(s32[6,128]{1,0:T(8,128)} %delay.1) | copy-start | bytes 9220
  138.7 202.6 %copy-start.10 = (f32[6,128]{1,0:T(8,128)S(1)}, f32[6,128]{1,0:T(8,128)}, u32[]{:S(2)}) copy-start(f32[6,128]{1,0:T(8,128)} %ydir.1) | copy-start | bytes 9220
  359.5 0.7 copy-start.16
  360.2 6.3 %copy-start.13 = (f32[16,8,256]{2,1,0:T(8,128)S(1)}, f32[16,8,256]{2,1,0:T(8,128)}, u32[]{:S(2)}) copy-start(f32[16,8,256]{2,1,0:T(8,128)} %get-tuple-element.477) | copy-start | bytes 393220 | tf_op jit(solution)/shard_map/cond

commit v2 on v0

--- a/solution.py
+++ b/solution.py
@@ -1,7 +1,511 @@
 import jax
 import jax.numpy as jnp
 from jax import lax
+from jax.experimental import pallas as pl
+from jax.experimental.pallas import tpu as pltpu
 from jax.sharding import PartitionSpec as P
+
+MESH = pl.DeviceIdType.MESH
+VMEM_CAP = 58 * 1024 * 1024
+DEVICES = 128
+SLOTS = 16
+ENDS = 256
+STEPS = 16
+F32 = jnp.float32
+BF16 = jnp.bfloat16
+RING = (0, 1, 2, 1)
+OFFSETS = sorted(
+    [(a, b, c, e) for a in range(4) for b in range(4) for c in range(4) for e in range(2) if (a, b, c, e) != (0, 0, 0, 0)],
+    key=lambda o: -(RING[o[0]] + RING[o[1]] + RING[o[2]] + 2 * o[3]),
+)
+
+
+def peer(i, z, offset):
+    dy, dx, dz, dc = offset
+    y, x, zz, c = i // 4, lax.rem(i, 4), z // 2, lax.rem(z, 2)
+    ni = lax.rem(y + dy, 4) * 4 + lax.rem(x + dx, 4)
+    nz = lax.rem(zz + dz, 4) * 2 + lax.rem(c + dc, 2)
+    return ni, nz
+
+
+def drain(ref, sem):
+    pltpu.make_async_copy(ref, ref, sem).wait()
+
+
+def split(value):
+    high = value.astype(BF16)
+    low = (value - high.astype(F32)).astype(BF16)
+    return high, low
+
+
+def dot_nt(left, right):
+    return lax.dot_general(left, right, (((1,), (1,)), ((), ())), preferred_element_type=F32)
+
+
+def iota(shape, dim):
+    return lax.broadcasted_iota(jnp.int32, shape, dim)
+
+
+def hot(condition):
+    return jnp.where(condition, 1.0, 0.0).astype(BF16)
+
+
+def steps_kernel(
+    inverses, sources, port_row, port_col, end_row, end_col, mmap_in, delay, waves, yd, yr, ydir, ys_in, pd, pr, ps_in,
+    volts_out, lines_out, flag_out,
+    yst, pst, yim, pim, hbuf, table, code_send, code_recv, table_send, table_recv, port_send, own_recv,
+    chunk, fixed, still, v0_send, v0, block, solve, mmap, hacc, cacc, ht, g,
+    to_peer, from_peer, to_line, from_line, wave_send, wave_recv, cur_send, cur_recv, inj,
+    code_sems, table_sems, port_sems, chunk_sem, v0_sems, block_sems, own_sem, wave_sems, cur_sems, inj_sems,
+):
+    i = lax.axis_index("net")
+    z = lax.axis_index("line")
+    me = i * 8 + z
+    lane = iota((1, 128), 1)
+    barrier = pltpu.get_barrier_semaphore()
+    for offset in OFFSETS:
+        pl.semaphore_signal(barrier, inc=1, device_id=peer(i, z, offset), device_id_type=MESH)
+
+    def send_all(src_of, dst, sends, recvs):
+        for offset in OFFSETS:
+            ni, nz = peer(i, z, offset)
+            pltpu.make_async_remote_copy(
+                src_ref=src_of(ni * 8 + nz), dst_ref=dst, send_sem=sends, recv_sem=recvs,
+                device_id=(ni, nz), device_id_type=MESH,
+            ).start()
+
+    def chunk_copy(c, slot):
+        return pltpu.make_async_copy(inverses.at[pl.ds(c * 4, 4)], chunk.at[slot], chunk_sem.at[slot])
+
+    chunk_copy(0, 0).start()
+
+    f = iota((1, ENDS), 1)
+    owner_dev = (i * 8 + f // 32).astype(F32)
+    owner_pos = (lax.rem(f // 8, 4) * 64 + z * 8 + lax.rem(f, 8)).astype(F32)
+    code_row = iota((128, ENDS), 0)
+    codes = jnp.where(
+        lax.rem(code_row, 8) == lax.rem(port_row[...], 8),
+        jnp.where(code_row < 8, owner_dev, jnp.where(code_row < 16, owner_pos, 0.0)), 0.0,
+    ).astype(BF16)
+    code_send[...] = dot_nt(hot(iota((DEVICES, ENDS), 0) == port_row[...] // 8), codes)[:, None, :]
+
+    pl.semaphore_wait(barrier, len(OFFSETS))
+    send_all(lambda d: code_send.at[d], code_recv.at[me], code_sems.at[0], code_sems.at[1])
+    code_recv[me] = code_send[me]
+
+    @pl.when(z < 3)
+    def _blocks():
+        for k in range(1, 8):
+            nz = lax.rem(z + k, 8)
+            pltpu.make_async_remote_copy(
+                src_ref=inverses.at[pl.ds(nz * 4, 4), :, pl.ds(0, 384)], dst_ref=block.at[z],
+                send_sem=block_sems.at[3], recv_sem=block_sems.at[z],
+                device_id=(i, nz), device_id_type=MESH,
+            ).start()
+        pltpu.make_async_copy(inverses.at[pl.ds(z * 4, 4), :, pl.ds(0, 384)], block.at[z], own_sem.at[0]).start()
+
+    table[...] = jnp.zeros(table.shape, F32)
+    yst[...] = ys_in[...]
+    pst[...] = ps_in[...]
+    yim[...] = yr[...]
+    pim[...] = pr[...]
+    depth = iota((6, 64, 128), 1)
+
+    def respond(n, carry):
+        pick = depth == (64 + n - delay[...])[:, None, :]
+        ydec, pdec, pres = yd[...], pd[...], pr[...]
+        for e in range(2):
+            seen = jnp.sum(jnp.where(pick, waves[1 - e], 0.0), axis=1)
+            now = pdec * pst[e] + pres * seen[:, None, :]
+            pst[e] = now
+            table[n, 0:6, e * 128:(e + 1) * 128] = jnp.sum(now, axis=1)
+            free = ydec * yst[e]
+            yst[e] = free
+            table[16 + n, 0:6, e * 128:(e + 1) * 128] = jnp.sum(free, axis=1)
+        first = jnp.where(n == 0, 1.0, 0.0)
+        pnow, ynow = pim[...], yim[...]
+        hbuf[n] = jnp.sum(pnow, axis=1)
+        gnow = jnp.sum(ynow, axis=1) + first * ydir[...]
+        table[48 + n, 0:6, 0:128] = gnow
+        table[48 + n, 0:6, 128:256] = gnow
+        pim[...] = pnow * pdec
+        yim[...] = ynow * ydec
+        return carry
+
+    lax.fori_loop(0, STEPS, respond, 0)
+    lag = delay[...]
+    for k in range(1, STEPS):
+        total = jnp.zeros((6, 128), F32)
+        for m in range(k):
+            total = total + jnp.where(lag == k - m, hbuf[m], 0.0)
+        table[32 + k, 0:6, 0:128] = total
+        table[32 + k, 0:6, 128:256] = total
+    for k in range(6):
+        for j in range(6):
+            m = k * 6 + j
+            row = mmap_in[k, j:j + 1, :]
+            table[m // 2, 6 + m % 2:7 + m % 2, 0:128] = row
+            table[m // 2, 6 + m % 2:7 + m % 2, 128:256] = row
+
+    drain(code_recv.at[pl.ds(0, DEVICES - 1)], code_sems.at[1])
+    got = code_recv[...].reshape(DEVICES, 128).astype(BF16)
+    found = jnp.dot(hot(iota((ENDS, DEVICES), 1) == end_col[...] // 8), got, preferred_element_type=F32)
+    code_lane = iota((ENDS, 128), 1)
+    found = jnp.where(
+        (lax.rem(code_lane, 8) == lax.rem(end_col[...], 8)) & (code_lane < 16), found, 0.0
+    ).astype(BF16)
+    end_owner = dot_nt(hot(iota((8, 128), 1) // 8 == iota((8, 128), 0)), found)
+    found_col = found.astype(F32)
+    end_dev_col = jnp.sum(jnp.where(code_lane < 8, found_col, 0.0), axis=1, keepdims=True)
+    end_pos_col = jnp.sum(jnp.where(code_lane >= 8, found_col, 0.0), axis=1, keepdims=True)
+    partner = jnp.concatenate([end_owner[0:2, 128:], end_owner[0:2, :128]], axis=1)
+    table[32, 0:2, :] = partner
+    table[32, 2:3, :] = jnp.full((1, ENDS), me).astype(F32)
+    table[32, 3:4, :] = f.astype(F32)
+
+    high, low = split(table[...].reshape(512, ENDS))
+    parts = jnp.concatenate([high, low], axis=0)
+
+    def fill(c, carry):
+        pick = hot(iota((256, ENDS), 0) + c * 256 == end_row[...])
+        rows = dot_nt(pick, parts)
+        table_send[pl.ds(c * 32, 32)] = (rows[:, :512] + rows[:, 512:]).reshape(32, 8, 512)
+        return carry
+
+    lax.fori_loop(0, 4, fill, 0)
+    send_all(lambda d: table_send.at[d], table_recv.at[me], table_sems.at[0], table_sems.at[1])
+    table_recv[me] = table_send[me]
+
+    def solve_sources(c, carry):
+        slot = lax.rem(c, 2)
+        chunk_copy(c, slot).wait()
+
+        @pl.when(c < 7)
+        def _next():
+            chunk_copy(c + 1, 1 - slot).start()
+
+        def one(s, carry):
+            a_high, a_low = split(chunk[slot, s])
+            matrix = jnp.concatenate([a_high, a_low], axis=0)
+            fixed[c * 4 + s] = matrix[:, :384]
+            s_high, s_low = split(sources[c * 4 + s])
+            both = dot_nt(jnp.concatenate([s_high, s_low], axis=0), matrix)
+            both = both[:STEPS] + both[STEPS:]
+            still[c * 4 + s] = both[:, :128] + both[:, 128:]
+            return carry
+
+        lax.fori_loop(0, 4, one, 0)
+        for t in range(2):
+            first, second = still[c * 4 + 2 * t], still[c * 4 + 2 * t + 1]
+            v0_send[c, t, :, 0:128] = jnp.where(lane < 64, first, pltpu.roll(second, 64, 1))
+            v0_send[c, t, :, 128:256] = jnp.where(lane < 64, pltpu.roll(first, 64, 1), second)
+
+        @pl.when((z < 3) & (c != z))
+        def _send():
+            pltpu.make_async_remote_copy(
+                src_ref=v0_send.at[c], dst_ref=v0.at[z], send_sem=v0_sems.at[3], recv_sem=v0_sems.at[z],
+                device_id=(i, c), device_id_type=MESH,
+            ).start()
+
+        @pl.when((z < 3) & (c == z))
+        def _keep():
+            v0[z] = v0_send[c]
+
+        return carry
+
+    lax.fori_loop(0, 8, solve_sources, 0)
+
+    drain(table_recv.at[pl.ds(0, DEVICES - 1)], table_sems.at[1])
+    at_port = jnp.zeros((ENDS, 1024), F32)
+    for c in range(4):
+        high, low = split(table_recv[c * 32:(c + 1) * 32].reshape(256, 512))
+        pick = hot(iota((ENDS, 256), 1) + c * 256 == port_col[...])
+        at_port = at_port + jnp.dot(pick, jnp.concatenate([high, low], axis=1), preferred_element_type=F32)
+    port_send[...] = (at_port[:, :512] + at_port[:, 512:]).reshape(8, 4, 8, 512)
+    for k in range(1, 8):
+        nz = lax.rem(z + k, 8)
+        pltpu.make_async_remote_copy(
+            src_ref=port_send.at[nz], dst_ref=own_recv.at[:, z], send_sem=port_sems.at[0], recv_sem=port_sems.at[1],
+            device_id=(i, nz), device_id_type=MESH,
+        ).start()
+    own_recv[:, z] = port_send[z]
+    drain(own_recv.at[:, pl.ds(0, 7)], port_sems.at[1])
+
+    mine = own_recv[...].reshape(ENDS, 512)
+    turned = mine.T.reshape(64, 8, ENDS)
+    real = iota((1, 8, ENDS), 1) < 6
+    hacc[...] = jnp.zeros(hacc.shape, F32)
+    cacc[...] = jnp.zeros(cacc.shape, F32)
+    hacc[0:STEPS] = jnp.where(real, turned[0:16], 0.0)
+    cacc[0:STEPS] = jnp.where(real, turned[16:32], 0.0)
+    ht[...] = jnp.where(real, turned[32:48], 0.0)
+    g[...] = jnp.where(real, turned[48:64], 0.0)
+    mmap[...] = jnp.zeros(mmap.shape, F32)
+    for k in range(6):
+        for j in range(6):
+            m = k * 6 + j
+            mmap[k, j:j + 1, :] = turned[m // 2, 6 + m % 2:7 + m % 2, :]
+
+    def rank_row(dev_row, dev_col):
+        before = (dev_row == dev_col) & (iota((ENDS, ENDS), 0) < iota((ENDS, ENDS), 1))
+        return jnp.sum(jnp.where(before, 1.0, 0.0), axis=0, keepdims=True).astype(jnp.int32)
+
+    def rank_col(dev_row, dev_col, pos_row, pos_col):
+        before = (dev_row == dev_col) & (pos_row < pos_col)
+        return jnp.sum(jnp.where(before, 1.0, 0.0), axis=1, keepdims=True).astype(jnp.int32)
+
+    peer_row, peer_col = turned[32, 0:1], mine[:, 256:257]
+    line_row, line_col = turned[32, 2:3], mine[:, 258:259]
+    peer_rank = rank_row(peer_row, peer_col)
+    line_rank = rank_row(line_row, line_col)
+    peer_rank_in = rank_col(peer_row, peer_col, turned[32, 1:2], mine[:, 257:258])
+    line_rank_in = rank_col(end_owner[0:1], end_dev_col, end_owner[1:2], end_pos_col)
+    to_peer[...] = hot(iota((DEVICES, ENDS), 0) == peer_row.astype(jnp.int32))
+    to_line[...] = hot(iota((DEVICES, ENDS), 0) == line_row.astype(jnp.int32))
+    from_peer[...] = hot(iota((ENDS, DEVICES), 1) == peer_col.astype(jnp.int32))
+    from_line[...] = hot(iota((ENDS, DEVICES), 1) == end_dev_col.astype(jnp.int32))
+    worst_rank = jnp.maximum(
+        jnp.max(peer_rank, axis=1, keepdims=True), jnp.max(line_rank, axis=1, keepdims=True)
+    )
+    over = jnp.where(worst_rank >= SLOTS, 1.0, 0.0)
+    flag_lane = jnp.where(lane == 127, 1.0, 0.0) * over
+    mode_pick = hot(lax.rem(iota((8, 256), 1), 128) // SLOTS == iota((8, 256), 0))
+
+    for src_z in range(3):
+        @pl.when(z != src_z)
+        def _wait():
+            drain(block.at[src_z], block_sems.at[src_z])
+            drain(v0.at[src_z], v0_sems.at[src_z])
+
+        @pl.when(z == src_z)
+        def _own():
+            drain(block.at[src_z], own_sem.at[0])
+
+    def build(t, carry):
+        for src_z in range(3):
+            for h in range(2):
+                for kk in range(2):
+                    rows = block[src_z, t * 2 + h, kk * 64:(kk + 1) * 64, :]
+                    row0 = (src_z * 2 + kk) * 128 + h * 64
+                    for k in range(6):
+                        tile = rows[:, (k // 2) * 128:(k // 2 + 1) * 128]
+                        if k % 2 != h:
+                            tile = pltpu.roll(tile, 64, 1)
+                        tile = jnp.where((lane // 64) == h, tile, 0.0)
+                        high, low = split(tile)
+                        solve[t, row0:row0 + 64, k * 128:(k + 1) * 128] = high
+                        solve[t, 768 + row0:768 + row0 + 64, k * 128:(k + 1) * 128] = low
+        return carry
+
+    lax.fori_loop(0, 2, build, 0)
+
+    def to_rows(values, rank, onehot):
+        spread = jnp.concatenate(
+            [jnp.broadcast_to(values[j:j + 1], (SLOTS, ENDS)) for j in range(6)]
+            + [jnp.zeros((2 * SLOTS, ENDS), F32)], axis=0
+        )
+        slot = lax.rem(iota((DEVICES, ENDS), 0), SLOTS)
+        high, low = split(jnp.where(slot == rank, spread, 0.0))
+        rows = dot_nt(onehot[...], jnp.concatenate([high, low], axis=0))
+        return rows[:, :128] + rows[:, 128:]
+
+    def from_rows(rows, rank, onehot):
+        high, low = split(rows)
+        found = jnp.dot(onehot[...], jnp.concatenate([high, low], axis=1), preferred_element_type=F32)
+        slot = lax.rem(iota((ENDS, 256), 1), SLOTS)
+        found = jnp.where(slot == rank, found, 0.0).astype(BF16)
+        return dot_nt(mode_pick, found)
+
+    def take_currents(n):
+        drain(cur_recv.at[n, pl.ds(0, DEVICES - 1)], cur_sems.at[n])
+        lines_out[n] = from_rows(cur_recv[n].reshape(DEVICES, 128), line_rank_in, from_line)
+
+    def step(n, carry):
+        delayed, worst = carry
+        hist = hacc[n] + ht[1] * delayed
+        phase = [jnp.sum(mmap[k] * hist, axis=0, keepdims=True) for k in range(6)]
+        volts = []
+        pieces = []
+        for t in range(2):
+            rows = [p[:, t * 128:(t + 1) * 128] for p in phase]
+            pieces += rows
+            high, low = split(jnp.concatenate(rows, axis=1))
+            both = dot_nt(jnp.concatenate([high, low], axis=0), solve[t])
+            total = jnp.sum(both, axis=0, keepdims=True)
+            total = total[:, :768] + total[:, 768:]
+            base = jnp.concatenate([v0[a, t, pl.ds(n, 1), :] for a in range(3)], axis=1)
+            volts.append(total + base)
+        inj[z, n, 0:12] = jnp.concatenate(pieces, axis=0)
+        modal = jnp.zeros((8, ENDS), F32)
+        for k in range(6):
+            row = jnp.concatenate([v[:, k * 128:(k + 1) * 128] for v in volts], axis=1)
+            modal = modal + mmap[k] * row
+        charac = cacc[n] + g[0] * modal
+        wave = 2.0 * charac - hist
+
+        @pl.when(n < STEPS - 1)
+        def _waves():
+            wave_send[n] = (to_rows(wave, peer_rank, to_peer) + flag_lane)[:, None, :]
+            send_all(lambda d: wave_send.at[n, d], wave_recv.at[n, me], wave_sems.at[0, n], wave_sems.at[1, n])
+            wave_recv[n, me] = wave_send[n, me]
+
+        cur_send[n] = to_rows(charac - hist, line_rank, to_line)[:, None, :]
+        send_all(lambda d: cur_send.at[n, d], cur_recv.at[n, me], cur_sems.at[STEPS + n], cur_sems.at[n])
+        cur_recv[n, me] = cur_send[n, me]
+        for k in range(1, 8):
+            nz = lax.rem(z + k, 8)
+            pltpu.make_async_remote_copy(
+                src_ref=inj.at[z, n], dst_ref=inj.at[z, n], send_sem=inj_sems.at[0], recv_sem=inj_sems.at[1],
+                device_id=(i, nz), device_id_type=MESH,
+            ).start()
+
+        for k in range(2, STEPS):
+            hacc[n + k - 1] = hacc[n + k - 1] + ht[k] * delayed
+        for k in range(1, STEPS):
+            cacc[n + k] = cacc[n + k] + g[k] * modal
+
+        @pl.when(n > 0)
+        def _lines():
+            take_currents(n - 1)
+
+        last = jnp.minimum(n, STEPS - 2)
+
+        @pl.when(n < STEPS - 1)
+        def _arrive():
+            drain(wave_recv.at[n, pl.ds(0, DEVICES - 1)], wave_sems.at[1, n])
+
+        rows = wave_recv[last].reshape(DEVICES, 128)
+        worst = jnp.maximum(worst, jnp.max(rows[:, 127:128], axis=0, keepdims=True))
+        return from_rows(rows, peer_rank_in, from_peer), worst
+
+    delayed, worst = lax.fori_loop(0, STEPS, step, (jnp.zeros((8, ENDS), F32), jnp.zeros((1, 1), F32)))
+    flag_out[...] = jnp.broadcast_to(worst, flag_out.shape)
+
+    drain(inj.at[pl.ds(0, 7)], inj_sems.at[1])
+
+    def finish(a, carry):
+        for t in range(2):
+            tiles = [inj[a, :, t * 6 + k, :] for k in range(6)]
+            for h in range(2):
+                s = a * 4 + t * 2 + h
+                left = []
+                for u in range(3):
+                    even, odd = tiles[2 * u], tiles[2 * u + 1]
+                    if h == 0:
+                        left.append(jnp.where(lane < 64, even, pltpu.roll(odd, 64, 1)))
+                    else:
+                        left.append(jnp.where(lane < 64, pltpu.roll(even, 64, 1), odd))
+                high, low = split(jnp.concatenate(left, axis=1))
+                both = dot_nt(jnp.concatenate([high, low], axis=0), fixed[s])
+                both = both[:STEPS] + both[STEPS:]
+                volts_out[s] = still[s] + both[:, :128] + both[:, 128:]
+        return carry
+
+    lax.fori_loop(0, 8, finish, 0)
+    take_currents(STEPS - 1)
+
+    drain(code_send.at[pl.ds(0, DEVICES - 1)], code_sems.at[0])
+    drain(table_send.at[pl.ds(0, DEVICES - 1)], table_sems.at[0])
+    drain(port_send.at[pl.ds(0, 7)], port_sems.at[0])
+    drain(inj.at[pl.ds(0, 7)], inj_sems.at[0])
+
+    def sent(n, carry):
+        drain(cur_send.at[n, pl.ds(0, DEVICES - 1)], cur_sems.at[STEPS + n])
+
+        @pl.when(n < STEPS - 1)
+        def _wave():
+            drain(wave_send.at[n, pl.ds(0, DEVICES - 1)], wave_sems.at[0, n])
+        return carry
+
+    lax.fori_loop(0, STEPS, sent, 0)
+
+    @pl.when(z < 3)
+    def _sent():
+        drain(v0_send.at[pl.ds(0, 7)], v0_sems.at[3])
+        drain(inverses.at[pl.ds(0, 28), :, pl.ds(0, 384)], block_sems.at[3])
+
+
+def run_steps(*operands):
+    vm = pl.BlockSpec(memory_space=pltpu.VMEM)
+    dma = pltpu.SemaphoreType.DMA
+    rows = (STEPS, DEVICES, 1, 128)
+    return pl.pallas_call(
+        steps_kernel,
+        out_shape=(
+            jax.ShapeDtypeStruct((32, STEPS, 128), F32),
+            jax.ShapeDtypeStruct((STEPS, 8, ENDS), F32),
+            jax.ShapeDtypeStruct((8, 128), F32),
+        ),
+        in_specs=[pl.BlockSpec(memory_space=pl.ANY)] + [vm] * (len(operands) - 1),
+        out_specs=(vm, vm, vm),
+        scratch_shapes=[
+            pltpu.VMEM((2, 6, 30, 128), F32),
+            pltpu.VMEM((2, 6, 30, 128), F32),
+            pltpu.VMEM((6, 30, 128), F32),
+            pltpu.VMEM((6, 30, 128), F32),
+            pltpu.VMEM((STEPS, 6, 128), F32),
+            pltpu.VMEM((64, 8, ENDS), F32),
+            pltpu.VMEM((DEVICES, 1, 128), F32),
+            pltpu.VMEM((DEVICES, 1, 128), F32),
+            pltpu.VMEM((DEVICES, 8, 512), F32),
+            pltpu.VMEM((DEVICES, 8, 512), F32),
+            pltpu.VMEM((8, 4, 8, 512), F32),
+            pltpu.VMEM((4, 8, 8, 512), F32),
+            pltpu.VMEM((2, 4, 128, 1024), F32),
+            pltpu.VMEM((32, 256, 384), BF16),
+            pltpu.VMEM((32, STEPS, 128), F32),
+            pltpu.VMEM((8, 2, STEPS, 256), F32),
+            pltpu.VMEM((3, 2, STEPS, 256), F32),
+            pltpu.VMEM((3, 4, 128, 384), F32),
+            pltpu.VMEM((2, 1536, 768), BF16),
+            pltpu.VMEM((6, 8, ENDS), F32),
+            pltpu.VMEM((32, 8, ENDS), F32),
+            pltpu.VMEM((32, 8, ENDS), F32),
+            pltpu.VMEM((STEPS, 8, ENDS), F32),
+            pltpu.VMEM((STEPS, 8, ENDS), F32),
+            pltpu.VMEM((DEVICES, ENDS), BF16),
+            pltpu.VMEM((ENDS, DEVICES), BF16),
+            pltpu.VMEM((DEVICES, ENDS), BF16),
+            pltpu.VMEM((ENDS, DEVICES), BF16),
+            pltpu.VMEM(rows, F32),
+            pltpu.VMEM(rows, F32),
+            pltpu.VMEM(rows, F32),
+            pltpu.VMEM(rows, F32),
+            pltpu.VMEM((8, STEPS, 16, 128), F32),
+            dma((2,)), dma((2,)), dma((2,)), dma((2,)), dma((4,)), dma((4,)), dma((1,)), dma((2, STEPS)),
+            dma((2 * STEPS,)), dma((2,)),
+        ],
+        compiler_params=pltpu.CompilerParams(collective_id=0, has_side_effects=True, vmem_limit_bytes=VMEM_CAP),
+        name="transient_steps",
+    )(*operands)
+
+
+def body(
+    inverses, node_counts, sources, port_slot, end_slot, modal_map, delay_steps, wave_buffer, yc_decay, yc_residue,
+    yc_direct, yc_state, prop_decay, prop_residue, prop_state,
+):
+    z = lax.axis_index("line")
+    port_flat = port_slot.reshape(-1)
+    end_flat = end_slot.reshape(-1)
+    volts, lines, flag = run_steps(
+        inverses, sources.transpose(1, 0, 2), port_flat[None, :], port_flat[:, None], end_flat[None, :],
+        end_flat[:, None], modal_map, delay_steps, wave_buffer, yc_decay, yc_residue, yc_direct, yc_state,
+        prop_decay, prop_residue, prop_state,
+    )
+
+    def quick(_):
+        row_ids = z * 128 + jnp.arange(128, dtype=jnp.int32)
+        live = row_ids[None, :] < node_counts[:, None]
+        ends = lines[:, :6].reshape(STEPS, 6, 2, 128)
+        return jnp.where(live[None], volts.transpose(1, 0, 2), 0.0), ends.transpose(0, 2, 1, 3)
+
+    def general(_):
+        return general_body(
+            inverses, node_counts, sources, port_slot, end_slot, modal_map, delay_steps, wave_buffer, yc_decay,
+            yc_residue, yc_direct, yc_state, prop_decay, prop_residue, prop_state,
+        )
+
+    return lax.cond(flag[0, 0] > 0.0, general, quick, 0)
 
 
 def read_delayed(extended, delay_steps, step_index, buffer_len):
@@ -21,7 +525,7 @@
     return arrived
 
 
-def body(
+def general_body(
     inverses,
     node_counts,
     sources,

time: 1480 us -> 262 us (0.18)
  waiting for transfers between devices: 438 us -> 0 us
  blocking collectives: 425 us -> 0 us
  matrix products: 263 us -> 0 us
  Pallas kernels: 0 us -> 246 us
  starting transfers between devices: 138 us -> 0 us
  local copies, waits for them, and re-layouts: 113 us -> 13.2 us
  other arithmetic: 100 us -> 0.89 us
    all_to_all x32 -> x0, waiting for transfers between devices: 438 us -> none  [the longest x16 219 us: move_back(): lax.all_to_all(outgoing, ('net', 'line'), split_axis=1, concat_axis=1, ti...]
    all_gather x32 -> x0, blocking collectives: 425 us -> none  [the longest x16 221 us: advance(): port_currents = lax.all_gather(own_ports, 'line', axis=1, tiled=True)]
    dot_general x16 -> x0, matrix products: 263 us -> none  [advance(): jnp.einsum('src,sc->sr', inverses, injection, precision=lax.Precision.HIG...]
    pallas_call x0 -> x1, Pallas kernels: none -> 246 us  [run_steps(): pl.pallas_call(steps_kernel, out_shape=(jax.ShapeDtypeStruct((32, STEPS,...]
    all_to_all x32 -> x0, starting transfers between devices: 138 us -> none  [the longest x16 80.7 us: move_back(): lax.all_to_all(outgoing, ('net', 'line'), split_axis=1, concat_axis=1, ti...]
    scatter x32 -> x0, local copies, waits for them, and re-layouts: 61.5 us -> none  [the longest x16 30.8 us: advance(): jnp.zeros((mode_count, slot_width), jnp.float32).at[:, port_flat]]
    reduce_sum x80 -> x0, other arithmetic: 41.7 us -> none  [the longest x16 19.4 us: advance(): history = jnp.sum(prop_now, axis=2)]
    gather x32 -> x0, local copies, waits for them, and re-layouts: 23.3 us -> none  [the longest x16 11.7 us: advance(): returned[:, port_flat].reshape(mode_count, sub_count, port_cols)]
  transfers between devices with their start and end apart: 32 -> 0, of which waited for: 32 -> 0; matrix products, arithmetic and copies ran while one was open for 0% -> 0% of each run, Pallas kernels for 0% -> 0%
where the time goes in v2:
time: 262 us
  Pallas kernels  246 us (94%)
  local copies, waits for them, and re-layouts  13.2 us (5%)
    pallas_call x1, Pallas kernels, run_steps(): pl.pallas_call(steps_kernel, out_shape=(jax.ShapeDtypeStruct((32, STEPS,...  246 us
    unnamed x30, local copies, waits for them, and re-layouts  8.42 us

profile of v2, /device:TPU:1, one launch (start us, length us, event | category | flops | bytes accessed | tf_op | source)
XLA Modules:
  0.0 261.9 jit_solution(3604452585159428276)
XLA Ops:
  0.6 0.0 copy-start.12
  0.6 0.0 copy-start.6
  0.7 0.0 copy-start.7
  0.7 0.0 copy-start.10
  0.7 0.0 copy-start.4
  0.7 0.0 copy-start.8
  0.7 0.0 copy-start.5
  0.7 0.0 copy-start
  0.7 0.0 copy-start.1
  0.7 0.0 copy-start.9
  0.7 0.0 copy-start.2
  0.8 0.0 copy-start.3
  0.8 0.0 copy-start.11
  0.8 0.9 copy.153
  1.7 0.7 broadcast_in_dim_reshape.16.port_col
  2.5 0.7 broadcast_in_dim_reshape.12.port_row
  3.1 4.2 %copy.189 = f32[16,32,1024]{2,0,1:T(8,128)} copy(f32[16,32,1024]{2,1,0:T(8,128)} %param.21) | data formatting | bytes 4194304 | tf_op args[2]
  7.3 1.6 copy.157.ys_in
  8.9 1.6 copy.158.ps_in
  10.5 1.5 copy.156.end_col
  12.0 246.2 %transient_steps.1 = (f32[32,16,128]{2,1,0:T(8,128)S(1)}, f32[16,8,256]{2,1,0:T(8,128)S(1)}, f32[8,128]{1,0:T(8,128)}) custom-call(f32[32,128,1024]{2,1,0:T(8,128)} %inverses.1, f32[32,16,1024]{2,1,0:T(8,128)} %bitcast.122, s32[1,256]{1,0:T(1,128)} %broadcast_in_dim_reshape.12.port_row, s32[256,1]{1,0:T(8,128)} %broadcast_in_dim_reshape.16.port_col, ...), custom_call_target="tpu_custom_call" | custom-call | tf_op jit(solution)/shard_map/transient_steps/pallas_call | solution.py:432
  258.2 1.2 slice.16
  260.0 0.0 copy-done.12
  260.0 0.0 copy-done.6
  260.0 0.0 copy-done.7
  260.0 0.0 copy-done.10
  260.1 0.0 copy-done.4
  260.1 0.0 copy-done.8
  260.1 0.0 copy-done.5
  260.1 0.0 copy-done
  260.1 0.0 copy-done.1
  260.1 0.0 copy-done.9
  260.1 0.0 copy-done.2
  260.1 0.0 copy-done.3
  260.1 0.0 copy-done.11
  260.1 1.7 conditional.1
  260.2 0.1 reshape.198
  260.3 0.7 copy.169
  261.0 0.1 broadcast_compare_fusion
  261.0 0.8 fusion.2
  (3 shorter events, 0.1 us)
Async XLA Ops:
  0.6 259.4 %copy-start.12 = (s32[32,8]{0,1:T(8,128)S(1)}, s32[32,8]{0,1:T(8,128)}, u32[]{:S(2)}) copy-start(s32[32,8]{0,1:T(8,128)} %param.22) | copy-start | bytes 3076
  0.6 259.4 %copy-start.6 = (f32[2,6,30,128]{3,0,2,1:T(2,128)S(1)}, f32[2,6,30,128]{3,0,2,1:T(2,128)}, u32[]{:S(2)}) copy-start(f32[2,6,30,128]{3,0,2,1:T(2,128)} %param.30) | copy-start | bytes 552964
  0.7 259.4 %copy-start.7 = (f32[2,6,30,128]{3,0,2,1:T(2,128)S(1)}, f32[2,6,30,128]{3,0,2,1:T(2,128)}, u32[]{:S(2)}) copy-start(f32[2,6,30,128]{3,0,2,1:T(2,128)} %param.33) | copy-start | bytes 552964
  0.7 259.4 %copy-start.10 = (s32[2,128]{1,0:T(2,128)S(1)}, s32[2,128]{1,0:T(2,128)}, u32[]{:S(2)}) copy-start(s32[2,128]{1,0:T(2,128)} %param.23) | copy-start | bytes 3076
  0.7 259.4 %copy-start.4 = (f32[6,6,128]{2,1,0:T(8,128)S(1)}, f32[6,6,128]{2,1,0:T(8,128)}, u32[]{:S(2)}) copy-start(f32[6,6,128]{2,1,0:T(8,128)} %mmap_in.1) | copy-start | bytes 55300
  0.7 259.4 %copy-start.8 = (s32[6,128]{1,0:T(8,128)S(1)}, s32[6,128]{1,0:T(8,128)}, u32[]{:S(2)}) copy-start(s32[6,128]{1,0:T(8,128)} %delay.1) | copy-start | bytes 9220
  0.7 259.4 %copy-start.5 = (f32[2,6,64,128]{3,2,1,0:T(8,128)S(1)}, f32[2,6,64,128]{3,2,1,0:T(8,128)}, u32[]{:S(2)}) copy-start(f32[2,6,64,128]{3,2,1,0:T(8,128)} %waves.1) | copy-start | bytes 1179652
  0.7 259.4 %copy-start = (f32[6,30,128]{2,1,0:T(8,128)S(1)}, f32[6,30,128]{2,1,0:T(8,128)}, u32[]{:S(2)}) copy-start(f32[6,30,128]{2,1,0:T(8,128)} %yd.1) | copy-start | bytes 276484
  0.7 259.4 %copy-start.1 = (f32[6,30,128]{2,1,0:T(8,128)S(1)}, f32[6,30,128]{2,1,0:T(8,128)}, u32[]{:S(2)}) copy-start(f32[6,30,128]{2,1,0:T(8,128)} %yr.1) | copy-start | bytes 276484
  0.7 259.4 %copy-start.9 = (f32[6,128]{1,0:T(8,128)S(1)}, f32[6,128]{1,0:T(8,128)}, u32[]{:S(2)}) copy-start(f32[6,128]{1,0:T(8,128)} %ydir.1) | copy-start | bytes 9220
  0.7 259.4 %copy-start.2 = (f32[6,30,128]{2,1,0:T(8,128)S(1)}, f32[6,30,128]{2,1,0:T(8,128)}, u32[]{:S(2)}) copy-start(f32[6,30,128]{2,1,0:T(8,128)} %pd.1) | copy-start | bytes 276484
  0.8 259.4 %copy-start.3 = (f32[6,30,128]{2,1,0:T(8,128)S(1)}, f32[6,30,128]{2,1,0:T(8,128)}, u32[]{:S(2)}) copy-start(f32[6,30,128]{2,1,0:T(8,128)} %pr.1) | copy-start | bytes 276484
  0.8 259.4 %copy-start.11 = (s32[32]{0:T(128)S(1)}, s32[32]{0:T(128)}, u32[]{:S(2)}) copy-start(s32[32]{0:T(128)} %param.20) | copy-start | bytes 388

commit v3 on v2

--- a/solution.py
+++ b/solution.py
@@ -51,12 +51,12 @@
 
 
 def steps_kernel(
-    inverses, sources, port_row, port_col, end_row, end_col, mmap_in, delay, waves, yd, yr, ydir, ys_in, pd, pr, ps_in,
+    inverses, counts, sources, port_row, end_row, mmap_in, delay, waves, yd, yr, ydir, ys_in, pd, pr, ps_in,
     volts_out, lines_out, flag_out,
     yst, pst, yim, pim, hbuf, table, code_send, code_recv, table_send, table_recv, port_send, own_recv,
-    chunk, fixed, still, v0_send, v0, block, solve, mmap, hacc, cacc, ht, g,
+    chunk, fixed, still, v0, block, relay, solve, mmap, hacc, cacc, ht, g,
     to_peer, from_peer, to_line, from_line, wave_send, wave_recv, cur_send, cur_recv, inj,
-    code_sems, table_sems, port_sems, chunk_sem, v0_sems, block_sems, own_sem, wave_sems, cur_sems, inj_sems,
+    code_sems, table_sems, port_sems, chunk_sem, v0_sems, block_sems, relay_sems, own_sem, wave_sems, cur_sems, inj_sems,
 ):
     i = lax.axis_index("net")
     z = lax.axis_index("line")
@@ -78,6 +78,12 @@
         return pltpu.make_async_copy(inverses.at[pl.ds(c * 4, 4)], chunk.at[slot], chunk_sem.at[slot])
 
     chunk_copy(0, 0).start()
+
+    def column(row):
+        return jnp.broadcast_to(row.astype(F32), (128, ENDS)).T[:, 0:1].astype(jnp.int32)
+
+    port_col = column(port_row[...])
+    end_col = column(end_row[...])
 
     f = iota((1, ENDS), 1)
     owner_dev = (i * 8 + f // 32).astype(F32)
@@ -93,20 +99,45 @@
     send_all(lambda d: code_send.at[d], code_recv.at[me], code_sems.at[0], code_sems.at[1])
     code_recv[me] = code_send[me]
 
+    chip, core = z // 2, lax.rem(z, 2)
+
+    def block_piece(dz, dc, first, count):
+        nz = lax.rem(chip + dz, 4) * 2 + lax.rem(core + dc, 2)
+        pltpu.make_async_remote_copy(
+            src_ref=inverses.at[pl.ds(nz * 4 + first, count), :, pl.ds(0, 384)],
+            dst_ref=block.at[z, pl.ds(first, count)], send_sem=block_sems.at[3], recv_sem=block_sems.at[z],
+            device_id=(i, nz), device_id_type=MESH,
+        ).start()
+
+    @pl.when(z < 2)
+    def _two_hops():
+        for dc in range(2):
+            nz = 4 + lax.rem(core + dc, 2)
+            pltpu.make_async_remote_copy(
+                src_ref=inverses.at[pl.ds(nz * 4 + 2, 2), :, pl.ds(0, 384)], dst_ref=relay.at[pl.ds(z * 2, 2)],
+                send_sem=block_sems.at[3], recv_sem=relay_sems.at[z],
+                device_id=(i, nz + 2), device_id_type=MESH,
+            ).start()
+            block_piece(2, dc, 0, 2)
+
+    @pl.when(z == 2)
+    def _two_hops_whole():
+        for dc in range(2):
+            nz = 6 + dc
+            pltpu.make_async_remote_copy(
+                src_ref=inverses.at[pl.ds(nz * 4, 4), :, pl.ds(0, 384)], dst_ref=relay,
+                send_sem=block_sems.at[3], recv_sem=relay_sems.at[0],
+                device_id=(i, nz - 2), device_id_type=MESH,
+            ).start()
+
     @pl.when(z < 3)
-    def _blocks():
-        for k in range(1, 8):
-            nz = lax.rem(z + k, 8)
-            pltpu.make_async_remote_copy(
-                src_ref=inverses.at[pl.ds(nz * 4, 4), :, pl.ds(0, 384)], dst_ref=block.at[z],
-                send_sem=block_sems.at[3], recv_sem=block_sems.at[z],
-                device_id=(i, nz), device_id_type=MESH,
-            ).start()
+    def _own():
         pltpu.make_async_copy(inverses.at[pl.ds(z * 4, 4), :, pl.ds(0, 384)], block.at[z], own_sem.at[0]).start()
 
     table[...] = jnp.zeros(table.shape, F32)
-    yst[...] = ys_in[...]
-    pst[...] = ps_in[...]
+    for e in range(2):
+        yst[e] = ys_in[:, :, e, :]
+        pst[e] = ps_in[:, :, e, :]
     yim[...] = yr[...]
     pim[...] = pr[...]
     depth = iota((6, 64, 128), 1)
@@ -149,10 +180,10 @@
 
     drain(code_recv.at[pl.ds(0, DEVICES - 1)], code_sems.at[1])
     got = code_recv[...].reshape(DEVICES, 128).astype(BF16)
-    found = jnp.dot(hot(iota((ENDS, DEVICES), 1) == end_col[...] // 8), got, preferred_element_type=F32)
+    found = jnp.dot(hot(iota((ENDS, DEVICES), 1) == end_col // 8), got, preferred_element_type=F32)
     code_lane = iota((ENDS, 128), 1)
     found = jnp.where(
-        (lax.rem(code_lane, 8) == lax.rem(end_col[...], 8)) & (code_lane < 16), found, 0.0
+        (lax.rem(code_lane, 8) == lax.rem(end_col, 8)) & (code_lane < 16), found, 0.0
     ).astype(BF16)
     end_owner = dot_nt(hot(iota((8, 128), 1) // 8 == iota((8, 128), 0)), found)
     found_col = found.astype(F32)
@@ -176,6 +207,12 @@
     send_all(lambda d: table_send.at[d], table_recv.at[me], table_sems.at[0], table_sems.at[1])
     table_recv[me] = table_send[me]
 
+    @pl.when(z < 3)
+    def _second_part():
+        block_piece(0, 1, 0, 4)
+        block_piece(1, 0, 0, 1)
+        block_piece(3, 0, 0, 1)
+
     def solve_sources(c, carry):
         slot = lax.rem(c, 2)
         chunk_copy(c, slot).wait()
@@ -188,38 +225,51 @@
             a_high, a_low = split(chunk[slot, s])
             matrix = jnp.concatenate([a_high, a_low], axis=0)
             fixed[c * 4 + s] = matrix[:, :384]
-            s_high, s_low = split(sources[c * 4 + s])
+            s_high, s_low = split(sources[:, pl.ds(c * 4 + s, 1), :].reshape(STEPS, 1024))
             both = dot_nt(jnp.concatenate([s_high, s_low], axis=0), matrix)
             both = both[:STEPS] + both[STEPS:]
             still[c * 4 + s] = both[:, :128] + both[:, 128:]
             return carry
 
         lax.fori_loop(0, 4, one, 0)
-        for t in range(2):
-            first, second = still[c * 4 + 2 * t], still[c * 4 + 2 * t + 1]
-            v0_send[c, t, :, 0:128] = jnp.where(lane < 64, first, pltpu.roll(second, 64, 1))
-            v0_send[c, t, :, 128:256] = jnp.where(lane < 64, pltpu.roll(first, 64, 1), second)
-
         @pl.when((z < 3) & (c != z))
         def _send():
             pltpu.make_async_remote_copy(
-                src_ref=v0_send.at[c], dst_ref=v0.at[z], send_sem=v0_sems.at[3], recv_sem=v0_sems.at[z],
+                src_ref=still.at[pl.ds(c * 4, 4)], dst_ref=v0.at[z], send_sem=v0_sems.at[3], recv_sem=v0_sems.at[z],
                 device_id=(i, c), device_id_type=MESH,
             ).start()
 
         @pl.when((z < 3) & (c == z))
         def _keep():
-            v0[z] = v0_send[c]
+            v0[z] = still[pl.ds(c * 4, 4)]
 
         return carry
 
     lax.fori_loop(0, 8, solve_sources, 0)
+
+    @pl.when(z >= 6)
+    def _relay():
+        for src_z in range(2):
+            part = relay.at[pl.ds(src_z * 2, 2)]
+            drain(part, relay_sems.at[src_z])
+            pltpu.make_async_remote_copy(
+                src_ref=part, dst_ref=block.at[src_z, pl.ds(2, 2)], send_sem=relay_sems.at[2],
+                recv_sem=block_sems.at[src_z], device_id=(i, z - 2), device_id_type=MESH,
+            ).start()
+
+    @pl.when((z == 4) | (z == 5))
+    def _relay_up():
+        drain(relay, relay_sems.at[0])
+        pltpu.make_async_remote_copy(
+            src_ref=relay, dst_ref=block.at[2], send_sem=relay_sems.at[2], recv_sem=block_sems.at[2],
+            device_id=(i, z + 2), device_id_type=MESH,
+        ).start()
 
     drain(table_recv.at[pl.ds(0, DEVICES - 1)], table_sems.at[1])
     at_port = jnp.zeros((ENDS, 1024), F32)
     for c in range(4):
         high, low = split(table_recv[c * 32:(c + 1) * 32].reshape(256, 512))
-        pick = hot(iota((ENDS, 256), 1) + c * 256 == port_col[...])
+        pick = hot(iota((ENDS, 256), 1) + c * 256 == port_col)
         at_port = at_port + jnp.dot(pick, jnp.concatenate([high, low], axis=1), preferred_element_type=F32)
     port_send[...] = (at_port[:, :512] + at_port[:, 512:]).reshape(8, 4, 8, 512)
     for k in range(1, 8):
@@ -229,6 +279,16 @@
             device_id=(i, nz), device_id_type=MESH,
         ).start()
     own_recv[:, z] = port_send[z]
+
+    @pl.when(z < 3)
+    def _third_part():
+        for first, count in ((1, 1), (2, 2)):
+            block_piece(1, 0, first, count)
+            block_piece(3, 0, first, count)
+        for first in (0, 2):
+            block_piece(1, 1, first, 2)
+            block_piece(3, 1, first, 2)
+
     drain(own_recv.at[:, pl.ds(0, 7)], port_sems.at[1])
 
     mine = own_recv[...].reshape(ENDS, 512)
@@ -281,23 +341,14 @@
         def _own():
             drain(block.at[src_z], own_sem.at[0])
 
-    def build(t, carry):
+    def build(sub, carry):
         for src_z in range(3):
-            for h in range(2):
-                for kk in range(2):
-                    rows = block[src_z, t * 2 + h, kk * 64:(kk + 1) * 64, :]
-                    row0 = (src_z * 2 + kk) * 128 + h * 64
-                    for k in range(6):
-                        tile = rows[:, (k // 2) * 128:(k // 2 + 1) * 128]
-                        if k % 2 != h:
-                            tile = pltpu.roll(tile, 64, 1)
-                        tile = jnp.where((lane // 64) == h, tile, 0.0)
-                        high, low = split(tile)
-                        solve[t, row0:row0 + 64, k * 128:(k + 1) * 128] = high
-                        solve[t, 768 + row0:768 + row0 + 64, k * 128:(k + 1) * 128] = low
+            high, low = split(block[src_z, sub])
+            solve[sub, src_z * 128:(src_z + 1) * 128] = high
+            solve[sub, 384 + src_z * 128:512 + src_z * 128] = low
         return carry
 
-    lax.fori_loop(0, 2, build, 0)
+    lax.fori_loop(0, 4, build, 0)
 
     def to_rows(values, rank, onehot):
         spread = jnp.concatenate(
@@ -318,27 +369,48 @@
 
     def take_currents(n):
         drain(cur_recv.at[n, pl.ds(0, DEVICES - 1)], cur_sems.at[n])
-        lines_out[n] = from_rows(cur_recv[n].reshape(DEVICES, 128), line_rank_in, from_line)
+        found = from_rows(cur_recv[n].reshape(DEVICES, 128), line_rank_in, from_line)
+        lines_out[n, 0] = found[0:6, 0:128]
+        lines_out[n, 1] = found[0:6, 128:256]
 
     def step(n, carry):
         delayed, worst = carry
         hist = hacc[n] + ht[1] * delayed
         phase = [jnp.sum(mmap[k] * hist, axis=0, keepdims=True) for k in range(6)]
-        volts = []
-        pieces = []
+        pieces = jnp.concatenate(
+            [p[:, t * 128:(t + 1) * 128] for t in range(2) for p in phase], axis=0
+        )
+        turned = pltpu.roll(pieces, 64, 1)
+        inj[z, n, 0:12] = pieces
+        tiles = []
         for t in range(2):
-            rows = [p[:, t * 128:(t + 1) * 128] for p in phase]
-            pieces += rows
-            high, low = split(jnp.concatenate(rows, axis=1))
-            both = dot_nt(jnp.concatenate([high, low], axis=0), solve[t])
-            total = jnp.sum(both, axis=0, keepdims=True)
-            total = total[:, :768] + total[:, 768:]
-            base = jnp.concatenate([v0[a, t, pl.ds(n, 1), :] for a in range(3)], axis=1)
-            volts.append(total + base)
-        inj[z, n, 0:12] = jnp.concatenate(pieces, axis=0)
+            for h in range(2):
+                even, odd = (turned, pieces) if h else (pieces, turned)
+                rows = [
+                    jnp.where(lane < 64, even[t * 6 + 2 * u:t * 6 + 2 * u + 1], odd[t * 6 + 2 * u + 1:t * 6 + 2 * u + 2])
+                    for u in range(3)
+                ]
+                high, low = split(jnp.concatenate(rows, axis=1))
+                both = dot_nt(jnp.concatenate([high, low], axis=0), solve[2 * t + h])
+                both = both[0:1] + both[1:2]
+                tiles += [
+                    both[:, u * 128:(u + 1) * 128] + both[:, 384 + u * 128:512 + u * 128]
+                    + v0[u, 2 * t + h, pl.ds(n, 1), :]
+                    for u in range(3)
+                ]
+        volts = jnp.concatenate(tiles, axis=0)
+        swung = pltpu.roll(volts, 64, 1)
         modal = jnp.zeros((8, ENDS), F32)
         for k in range(6):
-            row = jnp.concatenate([v[:, k * 128:(k + 1) * 128] for v in volts], axis=1)
+            left, right = (swung, volts) if k % 2 else (volts, swung)
+            row = jnp.concatenate(
+                [
+                    jnp.where(
+                        lane < 64, left[6 * t + k // 2:6 * t + k // 2 + 1], right[6 * t + 3 + k // 2:6 * t + 4 + k // 2]
+                    )
+                    for t in range(2)
+                ], axis=1
+            )
             modal = modal + mmap[k] * row
         charac = cacc[n] + g[0] * modal
         wave = 2.0 * charac - hist
@@ -352,12 +424,16 @@
         cur_send[n] = to_rows(charac - hist, line_rank, to_line)[:, None, :]
         send_all(lambda d: cur_send.at[n, d], cur_recv.at[n, me], cur_sems.at[STEPS + n], cur_sems.at[n])
         cur_recv[n, me] = cur_send[n, me]
-        for k in range(1, 8):
-            nz = lax.rem(z + k, 8)
-            pltpu.make_async_remote_copy(
-                src_ref=inj.at[z, n], dst_ref=inj.at[z, n], send_sem=inj_sems.at[0], recv_sem=inj_sems.at[1],
-                device_id=(i, nz), device_id_type=MESH,
-            ).start()
+
+        @pl.when(lax.rem(n, 4) == 3)
+        def _injections():
+            part = inj.at[z, pl.ds(n - 3, 4)]
+            for k in range(1, 8):
+                nz = lax.rem(z + k, 8)
+                pltpu.make_async_remote_copy(
+                    src_ref=part, dst_ref=part, send_sem=inj_sems.at[0], recv_sem=inj_sems.at[1],
+                    device_id=(i, nz), device_id_type=MESH,
+                ).start()
 
         for k in range(2, STEPS):
             hacc[n + k - 1] = hacc[n + k - 1] + ht[k] * delayed
@@ -379,7 +455,7 @@
         return from_rows(rows, peer_rank_in, from_peer), worst
 
     delayed, worst = lax.fori_loop(0, STEPS, step, (jnp.zeros((8, ENDS), F32), jnp.zeros((1, 1), F32)))
-    flag_out[...] = jnp.broadcast_to(worst, flag_out.shape)
+    flag_out[...] = worst
 
     drain(inj.at[pl.ds(0, 7)], inj_sems.at[1])
 
@@ -398,7 +474,9 @@
                 high, low = split(jnp.concatenate(left, axis=1))
                 both = dot_nt(jnp.concatenate([high, low], axis=0), fixed[s])
                 both = both[:STEPS] + both[STEPS:]
-                volts_out[s] = still[s] + both[:, :128] + both[:, 128:]
+                total = still[s] + both[:, :128] + both[:, 128:]
+                live = lane + z * 128 < counts[s]
+                volts_out[:, pl.ds(s, 1), :] = jnp.where(live, total, 0.0)[:, None, :]
         return carry
 
     lax.fori_loop(0, 8, finish, 0)
@@ -419,9 +497,13 @@
 
     lax.fori_loop(0, STEPS, sent, 0)
 
+    @pl.when(z >= 4)
+    def _relayed():
+        drain(relay, relay_sems.at[2])
+
     @pl.when(z < 3)
     def _sent():
-        drain(v0_send.at[pl.ds(0, 7)], v0_sems.at[3])
+        drain(still.at[pl.ds(0, 28)], v0_sems.at[3])
         drain(inverses.at[pl.ds(0, 28), :, pl.ds(0, 384)], block_sems.at[3])
 
 
@@ -432,11 +514,11 @@
     return pl.pallas_call(
         steps_kernel,
         out_shape=(
-            jax.ShapeDtypeStruct((32, STEPS, 128), F32),
-            jax.ShapeDtypeStruct((STEPS, 8, ENDS), F32),
-            jax.ShapeDtypeStruct((8, 128), F32),
+            jax.ShapeDtypeStruct((STEPS, 32, 128), F32),
+            jax.ShapeDtypeStruct((STEPS, 2, 6, 128), F32),
+            jax.ShapeDtypeStruct((1, 1), F32),
         ),
-        in_specs=[pl.BlockSpec(memory_space=pl.ANY)] + [vm] * (len(operands) - 1),
+        in_specs=[pl.BlockSpec(memory_space=pl.ANY), pl.BlockSpec(memory_space=pltpu.SMEM)] + [vm] * (len(operands) - 2),
         out_specs=(vm, vm, vm),
         scratch_shapes=[
             pltpu.VMEM((2, 6, 30, 128), F32),
@@ -454,10 +536,10 @@
             pltpu.VMEM((2, 4, 128, 1024), F32),
             pltpu.VMEM((32, 256, 384), BF16),
             pltpu.VMEM((32, STEPS, 128), F32),
-            pltpu.VMEM((8, 2, STEPS, 256), F32),
-            pltpu.VMEM((3, 2, STEPS, 256), F32),
+            pltpu.VMEM((3, 4, STEPS, 128), F32),
             pltpu.VMEM((3, 4, 128, 384), F32),
-            pltpu.VMEM((2, 1536, 768), BF16),
+            pltpu.VMEM((4, 128, 384), F32),
+            pltpu.VMEM((4, 768, 384), BF16),
             pltpu.VMEM((6, 8, ENDS), F32),
             pltpu.VMEM((32, 8, ENDS), F32),
             pltpu.VMEM((32, 8, ENDS), F32),
@@ -472,7 +554,7 @@
             pltpu.VMEM(rows, F32),
             pltpu.VMEM(rows, F32),
             pltpu.VMEM((8, STEPS, 16, 128), F32),
-            dma((2,)), dma((2,)), dma((2,)), dma((2,)), dma((4,)), dma((4,)), dma((1,)), dma((2, STEPS)),
+            dma((2,)), dma((2,)), dma((2,)), dma((2,)), dma((4,)), dma((4,)), dma((3,)), dma((1,)), dma((2, STEPS)),
             dma((2 * STEPS,)), dma((2,)),
         ],
         compiler_params=pltpu.CompilerParams(collective_id=0, has_side_effects=True, vmem_limit_bytes=VMEM_CAP),
@@ -484,20 +566,14 @@
     inverses, node_counts, sources, port_slot, end_slot, modal_map, delay_steps, wave_buffer, yc_decay, yc_residue,
     yc_direct, yc_state, prop_decay, prop_residue, prop_state,
 ):
-    z = lax.axis_index("line")
-    port_flat = port_slot.reshape(-1)
-    end_flat = end_slot.reshape(-1)
     volts, lines, flag = run_steps(
-        inverses, sources.transpose(1, 0, 2), port_flat[None, :], port_flat[:, None], end_flat[None, :],
-        end_flat[:, None], modal_map, delay_steps, wave_buffer, yc_decay, yc_residue, yc_direct, yc_state,
-        prop_decay, prop_residue, prop_state,
+        inverses, node_counts, sources, port_slot.reshape(1, -1), end_slot.reshape(1, -1), modal_map, delay_steps,
+        wave_buffer, yc_decay, yc_residue, yc_direct, yc_state.transpose(1, 2, 0, 3), prop_decay, prop_residue,
+        prop_state.transpose(1, 2, 0, 3),
     )
 
     def quick(_):
-        row_ids = z * 128 + jnp.arange(128, dtype=jnp.int32)
-        live = row_ids[None, :] < node_counts[:, None]
-        ends = lines[:, :6].reshape(STEPS, 6, 2, 128)
-        return jnp.where(live[None], volts.transpose(1, 0, 2), 0.0), ends.transpose(0, 2, 1, 3)
+        return volts, lines
 
     def general(_):
         return general_body(

time: 262 us -> 228 us (0.87)
  Pallas kernels: 246 us -> 222 us
  local copies, waits for them, and re-layouts: 13.2 us -> 4.05 us
    pallas_call x1, Pallas kernels: 246 us -> 222 us  [run_steps(): pl.pallas_call(steps_kernel, out_shape=(jax.ShapeDtypeStruct((STEPS, 32,...]
    unnamed x30 -> x28, local copies, waits for them, and re-layouts: 8.42 us -> 2.7 us
    another operation x4 -> x0, local copies, waits for them, and re-layouts: 2.89 us -> none  [the longest x1 1.45 us: body(): end_flat[:, None]]
where the time goes in v3:
time: 228 us; the launch traced here: 227 us
  Pallas kernels  222 us (97%)
  local copies, waits for them, and re-layouts  4.05 us (2%)
    pallas_call x1, Pallas kernels, run_steps(): pl.pallas_call(steps_kernel, out_shape=(jax.ShapeDtypeStruct((STEPS, 32,...  222 us

profile of v3, /device:TPU:1, one launch (start us, length us, event | category | flops | bytes accessed | tf_op | source)
XLA Modules:
  0.0 227.4 jit_solution(5133198482514531486)
XLA Ops:
  0.6 0.0 copy-start.7
  0.6 0.0 copy-start.3
  0.7 0.0 copy-start.2
  0.7 0.0 copy-start.6
  0.7 0.0 copy-start.9
  0.7 0.0 copy-start.1
  0.7 0.0 copy-start
  0.7 0.0 copy-start.5
  0.7 0.0 copy-start.8
  0.7 0.0 copy-start.4
  0.8 0.0 copy-start.10
  0.8 0.0 copy-start.12
  0.8 0.0 copy-start.11
  0.8 1.0 copy.95
  1.7 0.7 reshape.183.port_row
  2.4 221.8 %transient_steps.1 = (f32[16,32,128]{2,1,0:T(8,128)}, f32[16,2,6,128]{3,2,1,0:T(8,128)S(1)}, f32[1,1]{1,0:T(1,128)}) custom-call(f32[32,128,1024]{2,1,0:T(8,128)} %inverses.1, s32[32]{0:T(128)} %counts.1, f32[16,32,1024]{2,1,0:T(8,128)} %sources.1, s32[1,256]{1,0:T(1,128)} %reshape.183.port_row, s32[1,256]{1,0:T(1,128)} %bitcast.133, f32[6,6,128]{2,1,0:T(8,128)} %mmap_in.1, ...), custom_call_target="tpu_custom_call" | custom-call | tf_op jit(solution)/shard_map/transient_steps/pallas_call | solution.py:514
  224.9 0.0 copy-done.7
  224.9 0.0 copy-done.3
  224.9 0.0 copy-done.2
  224.9 0.0 copy-done.6
  224.9 0.0 copy-done.9
  224.9 0.0 copy-done.1
  224.9 0.0 copy-done
  224.9 0.0 copy-done.5
  225.0 0.0 copy-done.8
  225.0 0.0 copy-done.4
  225.0 0.0 copy-done.10
  225.0 0.0 copy-done.12
  225.0 0.0 copy-done.11
  225.0 0.7 conditional.1
  225.0 0.7 copy.104
  225.7 1.7 copy.177
Async XLA Ops:
  0.6 224.3 %copy-start.7 = (f32[2,6,30,128]{3,0,2,1:T(2,128)S(1)}, f32[2,6,30,128]{3,0,2,1:T(2,128)}, u32[]{:S(2)}) copy-start(f32[2,6,30,128]{3,0,2,1:T(2,128)} %param.33) | copy-start | bytes 552964
  0.6 224.3 %copy-start.3 = (f32[6,30,128]{2,1,0:T(8,128)S(1)}, f32[6,30,128]{2,1,0:T(8,128)}, u32[]{:S(2)}) copy-start(f32[6,30,128]{2,1,0:T(8,128)} %pr.1) | copy-start | bytes 276484
  0.7 224.2 %copy-start.2 = (f32[6,30,128]{2,1,0:T(8,128)S(1)}, f32[6,30,128]{2,1,0:T(8,128)}, u32[]{:S(2)}) copy-start(f32[6,30,128]{2,1,0:T(8,128)} %pd.1) | copy-start | bytes 276484
  0.7 224.2 %copy-start.6 = (f32[2,6,30,128]{3,0,2,1:T(2,128)S(1)}, f32[2,6,30,128]{3,0,2,1:T(2,128)}, u32[]{:S(2)}) copy-start(f32[2,6,30,128]{3,0,2,1:T(2,128)} %param.30) | copy-start | bytes 552964
  0.7 224.2 %copy-start.9 = (f32[6,128]{1,0:T(8,128)S(1)}, f32[6,128]{1,0:T(8,128)}, u32[]{:S(2)}) copy-start(f32[6,128]{1,0:T(8,128)} %ydir.1) | copy-start | bytes 9220
  0.7 224.2 %copy-start.1 = (f32[6,30,128]{2,1,0:T(8,128)S(1)}, f32[6,30,128]{2,1,0:T(8,128)}, u32[]{:S(2)}) copy-start(f32[6,30,128]{2,1,0:T(8,128)} %yr.1) | copy-start | bytes 276484
  0.7 224.2 %copy-start = (f32[6,30,128]{2,1,0:T(8,128)S(1)}, f32[6,30,128]{2,1,0:T(8,128)}, u32[]{:S(2)}) copy-start(f32[6,30,128]{2,1,0:T(8,128)} %yd.1) | copy-start | bytes 276484
  0.7 224.2 %copy-start.5 = (f32[2,6,64,128]{3,2,1,0:T(8,128)S(1)}, f32[2,6,64,128]{3,2,1,0:T(8,128)}, u32[]{:S(2)}) copy-start(f32[2,6,64,128]{3,2,1,0:T(8,128)} %waves.1) | copy-start | bytes 1179652
  0.7 224.2 %copy-start.8 = (s32[6,128]{1,0:T(8,128)S(1)}, s32[6,128]{1,0:T(8,128)}, u32[]{:S(2)}) copy-start(s32[6,128]{1,0:T(8,128)} %delay.1) | copy-start | bytes 9220
  0.7 224.2 %copy-start.4 = (f32[6,6,128]{2,1,0:T(8,128)S(1)}, f32[6,6,128]{2,1,0:T(8,128)}, u32[]{:S(2)}) copy-start(f32[6,6,128]{2,1,0:T(8,128)} %mmap_in.1) | copy-start | bytes 55300
  0.8 224.2 %copy-start.10 = (s32[2,128]{1,0:T(2,128)S(1)}, s32[2,128]{1,0:T(2,128)}, u32[]{:S(2)}) copy-start(s32[2,128]{1,0:T(2,128)} %param.23) | copy-start | bytes 3076
  0.8 224.2 %copy-start.12 = (s32[32,8]{0,1:T(8,128)S(1)}, s32[32,8]{0,1:T(8,128)}, u32[]{:S(2)}) copy-start(s32[32,8]{0,1:T(8,128)} %param.22) | copy-start | bytes 3076
  0.8 224.2 %copy-start.11 = (s32[32]{0:T(128)S(1)}, s32[32]{0:T(128)}, u32[]{:S(2)}) copy-start(s32[32]{0:T(128)} %counts.1) | copy-start | bytes 388

commit v4 on v3

--- a/solution.py
+++ b/solution.py
@@ -9,6 +9,7 @@
 VMEM_CAP = 58 * 1024 * 1024
 DEVICES = 128
 SLOTS = 16
+PACK = 64
 ENDS = 256
 STEPS = 16
 F32 = jnp.float32
@@ -82,7 +83,6 @@
     def column(row):
         return jnp.broadcast_to(row.astype(F32), (128, ENDS)).T[:, 0:1].astype(jnp.int32)
 
-    port_col = column(port_row[...])
     end_col = column(end_row[...])
 
     f = iota((1, ENDS), 1)
@@ -193,6 +193,8 @@
     table[32, 0:2, :] = partner
     table[32, 2:3, :] = jnp.full((1, ENDS), me).astype(F32)
     table[32, 3:4, :] = f.astype(F32)
+    table[32, 4:6, :] = end_owner[0:2]
+    table[32, 6:7, :] = jnp.ones((1, ENDS), F32)
 
     high, low = split(table[...].reshape(512, ENDS))
     parts = jnp.concatenate([high, low], axis=0)
@@ -204,14 +206,19 @@
         return carry
 
     lax.fori_loop(0, 4, fill, 0)
-    send_all(lambda d: table_send.at[d], table_recv.at[me], table_sems.at[0], table_sems.at[1])
-    table_recv[me] = table_send[me]
+    for dy, dx in sorted([(a, b) for a in range(4) for b in range(4)], key=lambda o: -(RING[o[0]] + RING[o[1]]))[:15]:
+        ni, _ = peer(i, z, (dy, dx, 0, 0))
+        pltpu.make_async_remote_copy(
+            src_ref=table_send.at[pl.ds(ni * 8, 8)], dst_ref=table_recv.at[pl.ds(i * 8, 8)],
+            send_sem=table_sems.at[0], recv_sem=table_sems.at[1], device_id=(ni, z), device_id_type=MESH,
+        ).start()
+    table_recv[pl.ds(i * 8, 8)] = table_send[pl.ds(i * 8, 8)]
 
     @pl.when(z < 3)
     def _second_part():
         block_piece(0, 1, 0, 4)
-        block_piece(1, 0, 0, 1)
-        block_piece(3, 0, 0, 1)
+        block_piece(1, 0, 0, 4)
+        block_piece(3, 0, 0, 4)
 
     def solve_sources(c, carry):
         slot = lax.rem(c, 2)
@@ -265,33 +272,52 @@
             device_id=(i, z + 2), device_id_type=MESH,
         ).start()
 
-    drain(table_recv.at[pl.ds(0, DEVICES - 1)], table_sems.at[1])
-    at_port = jnp.zeros((ENDS, 1024), F32)
+    meta_pick = hot(iota((8, 512), 1) == 256 + iota((8, 512), 0))
+    drain(table_recv.at[pl.ds(0, DEVICES - 8)], table_sems.at[1])
+    meta = jnp.concatenate(
+        [dot_nt(meta_pick, table_recv[c * 32:(c + 1) * 32].reshape(256, 512).astype(BF16)) for c in range(4)], axis=1
+    )
+    target = (meta[4:5].astype(jnp.int32) - i * 8)
+    held = meta[6:7] > 0.5
+    chosen = (iota((8, 1024), 0) == target) & held
+    chosen_hot = hot(chosen)
+    ahead = jnp.concatenate(
+        [
+            jnp.dot(chosen_hot, hot(iota((1024, 256), 0) < iota((1024, 256), 1) + c * 256), preferred_element_type=F32)
+            for c in range(4)
+        ], axis=1
+    )
+    place = jnp.sum(jnp.where(chosen, ahead, 0.0), axis=0, keepdims=True).astype(jnp.int32)
+    pack_over = jnp.max(place, axis=1, keepdims=True) >= PACK
+    key = jnp.where(held & (place < PACK), target * PACK + place, -1)
+    packed = jnp.zeros((8 * PACK, 1024), F32)
     for c in range(4):
         high, low = split(table_recv[c * 32:(c + 1) * 32].reshape(256, 512))
-        pick = hot(iota((ENDS, 256), 1) + c * 256 == port_col)
-        at_port = at_port + jnp.dot(pick, jnp.concatenate([high, low], axis=1), preferred_element_type=F32)
-    port_send[...] = (at_port[:, :512] + at_port[:, 512:]).reshape(8, 4, 8, 512)
+        pick = hot(iota((8 * PACK, 256), 0) == key[:, c * 256:(c + 1) * 256])
+        packed = packed + jnp.dot(pick, jnp.concatenate([high, low], axis=1), preferred_element_type=F32)
+    port_send[...] = (packed[:, :512] + packed[:, 512:]).reshape(8, PACK, 512)
     for k in range(1, 8):
         nz = lax.rem(z + k, 8)
         pltpu.make_async_remote_copy(
-            src_ref=port_send.at[nz], dst_ref=own_recv.at[:, z], send_sem=port_sems.at[0], recv_sem=port_sems.at[1],
+            src_ref=port_send.at[nz], dst_ref=own_recv.at[z], send_sem=port_sems.at[0], recv_sem=port_sems.at[1],
             device_id=(i, nz), device_id_type=MESH,
         ).start()
-    own_recv[:, z] = port_send[z]
+    own_recv[z] = port_send[z]
 
     @pl.when(z < 3)
     def _third_part():
-        for first, count in ((1, 1), (2, 2)):
-            block_piece(1, 0, first, count)
-            block_piece(3, 0, first, count)
         for first in (0, 2):
             block_piece(1, 1, first, 2)
             block_piece(3, 1, first, 2)
 
-    drain(own_recv.at[:, pl.ds(0, 7)], port_sems.at[1])
-
-    mine = own_recv[...].reshape(ENDS, 512)
+    drain(own_recv.at[pl.ds(0, 7)], port_sems.at[1])
+
+    high, low = split(own_recv[...].reshape(8 * PACK, 512))
+    meta = dot_nt(meta_pick, high)
+    spot = jnp.where(meta[6:7] > 0.5, meta[5:6].astype(jnp.int32), -1)
+    pick = hot(iota((ENDS, 8 * PACK), 0) == spot)
+    mine = jnp.dot(pick, jnp.concatenate([high, low], axis=1), preferred_element_type=F32)
+    mine = mine[:, :512] + mine[:, 512:]
     turned = mine.T.reshape(64, 8, ENDS)
     real = iota((1, 8, ENDS), 1) < 6
     hacc[...] = jnp.zeros(hacc.shape, F32)
@@ -327,7 +353,7 @@
     worst_rank = jnp.maximum(
         jnp.max(peer_rank, axis=1, keepdims=True), jnp.max(line_rank, axis=1, keepdims=True)
     )
-    over = jnp.where(worst_rank >= SLOTS, 1.0, 0.0)
+    over = jnp.where((worst_rank >= SLOTS) | pack_over, 1.0, 0.0)
     flag_lane = jnp.where(lane == 127, 1.0, 0.0) * over
     mode_pick = hot(lax.rem(iota((8, 256), 1), 128) // SLOTS == iota((8, 256), 0))
 
@@ -483,7 +509,7 @@
     take_currents(STEPS - 1)
 
     drain(code_send.at[pl.ds(0, DEVICES - 1)], code_sems.at[0])
-    drain(table_send.at[pl.ds(0, DEVICES - 1)], table_sems.at[0])
+    drain(table_send.at[pl.ds(0, DEVICES - 8)], table_sems.at[0])
     drain(port_send.at[pl.ds(0, 7)], port_sems.at[0])
     drain(inj.at[pl.ds(0, 7)], inj_sems.at[0])
 
@@ -531,8 +557,8 @@
             pltpu.VMEM((DEVICES, 1, 128), F32),
             pltpu.VMEM((DEVICES, 8, 512), F32),
             pltpu.VMEM((DEVICES, 8, 512), F32),
-            pltpu.VMEM((8, 4, 8, 512), F32),
-            pltpu.VMEM((4, 8, 8, 512), F32),
+            pltpu.VMEM((8, PACK, 512), F32),
+            pltpu.VMEM((8, PACK, 512), F32),
             pltpu.VMEM((2, 4, 128, 1024), F32),
             pltpu.VMEM((32, 256, 384), BF16),
             pltpu.VMEM((32, STEPS, 128), F32),

time: 228 us -> 212 us (0.930)
  Pallas kernels: 222 us -> 206 us
    pallas_call x1, Pallas kernels: 222 us -> 206 us  [run_steps(): pl.pallas_call(steps_kernel, out_shape=(jax.ShapeDtypeStruct((STEPS, 32,...]
where the time goes in v4:
time: 212 us
  Pallas kernels  206 us (97%)
  local copies, waits for them, and re-layouts  4.05 us (2%)
    pallas_call x1, Pallas kernels, run_steps(): pl.pallas_call(steps_kernel, out_shape=(jax.ShapeDtypeStruct((STEPS, 32,...  206 us

profile of v4, /device:TPU:1, one launch (start us, length us, event | category | flops | bytes accessed | tf_op | source)
XLA Modules:
  0.0 211.5 jit_solution(11084846232990233556)
XLA Ops:
  0.6 0.0 copy-start.7
  0.6 0.0 copy-start.3
  0.7 0.0 copy-start.2
  0.7 0.0 copy-start.6
  0.7 0.0 copy-start.9
  0.7 0.0 copy-start.1
  0.7 0.0 copy-start
  0.7 0.0 copy-start.5
  0.7 0.0 copy-start.8
  0.7 0.0 copy-start.4
  0.8 0.0 copy-start.10
  0.8 0.0 copy-start.12
  0.8 0.0 copy-start.11
  0.8 1.0 copy.95
  1.7 0.7 reshape.183.port_row
  2.4 205.9 %transient_steps.1 = (f32[16,32,128]{2,1,0:T(8,128)}, f32[16,2,6,128]{3,2,1,0:T(8,128)S(1)}, f32[1,1]{1,0:T(1,128)}) custom-call(f32[32,128,1024]{2,1,0:T(8,128)} %inverses.1, s32[32]{0:T(128)} %counts.1, f32[16,32,1024]{2,1,0:T(8,128)} %sources.1, s32[1,256]{1,0:T(1,128)} %reshape.183.port_row, s32[1,256]{1,0:T(1,128)} %bitcast.133, f32[6,6,128]{2,1,0:T(8,128)} %mmap_in.1, ...), custom_call_target="tpu_custom_call" | custom-call | tf_op jit(solution)/shard_map/transient_steps/pallas_call | solution.py:540
  209.0 0.0 copy-done.7
  209.0 0.0 copy-done.3
  209.0 0.0 copy-done.2
  209.0 0.0 copy-done.6
  209.0 0.0 copy-done.9
  209.1 0.0 copy-done.1
  209.1 0.0 copy-done
  209.1 0.0 copy-done.5
  209.1 0.0 copy-done.8
  209.1 0.0 copy-done.4
  209.1 0.0 copy-done.10
  209.1 0.0 copy-done.12
  209.1 0.0 copy-done.11
  209.1 0.7 conditional.1
  209.1 0.7 copy.104
  209.8 1.7 copy.177
Async XLA Ops:
  0.6 208.4 %copy-start.7 = (f32[2,6,30,128]{3,0,2,1:T(2,128)S(1)}, f32[2,6,30,128]{3,0,2,1:T(2,128)}, u32[]{:S(2)}) copy-start(f32[2,6,30,128]{3,0,2,1:T(2,128)} %param.33) | copy-start | bytes 552964
  0.6 208.4 %copy-start.3 = (f32[6,30,128]{2,1,0:T(8,128)S(1)}, f32[6,30,128]{2,1,0:T(8,128)}, u32[]{:S(2)}) copy-start(f32[6,30,128]{2,1,0:T(8,128)} %pr.1) | copy-start | bytes 276484
  0.7 208.4 %copy-start.2 = (f32[6,30,128]{2,1,0:T(8,128)S(1)}, f32[6,30,128]{2,1,0:T(8,128)}, u32[]{:S(2)}) copy-start(f32[6,30,128]{2,1,0:T(8,128)} %pd.1) | copy-start | bytes 276484
  0.7 208.4 %copy-start.6 = (f32[2,6,30,128]{3,0,2,1:T(2,128)S(1)}, f32[2,6,30,128]{3,0,2,1:T(2,128)}, u32[]{:S(2)}) copy-start(f32[2,6,30,128]{3,0,2,1:T(2,128)} %param.30) | copy-start | bytes 552964
  0.7 208.4 %copy-start.9 = (f32[6,128]{1,0:T(8,128)S(1)}, f32[6,128]{1,0:T(8,128)}, u32[]{:S(2)}) copy-start(f32[6,128]{1,0:T(8,128)} %ydir.1) | copy-start | bytes 9220
  0.7 208.4 %copy-start.1 = (f32[6,30,128]{2,1,0:T(8,128)S(1)}, f32[6,30,128]{2,1,0:T(8,128)}, u32[]{:S(2)}) copy-start(f32[6,30,128]{2,1,0:T(8,128)} %yr.1) | copy-start | bytes 276484
  0.7 208.4 %copy-start = (f32[6,30,128]{2,1,0:T(8,128)S(1)}, f32[6,30,128]{2,1,0:T(8,128)}, u32[]{:S(2)}) copy-start(f32[6,30,128]{2,1,0:T(8,128)} %yd.1) | copy-start | bytes 276484
  0.7 208.4 %copy-start.5 = (f32[2,6,64,128]{3,2,1,0:T(8,128)S(1)}, f32[2,6,64,128]{3,2,1,0:T(8,128)}, u32[]{:S(2)}) copy-start(f32[2,6,64,128]{3,2,1,0:T(8,128)} %waves.1) | copy-start | bytes 1179652
  0.7 208.4 %copy-start.8 = (s32[6,128]{1,0:T(8,128)S(1)}, s32[6,128]{1,0:T(8,128)}, u32[]{:S(2)}) copy-start(s32[6,128]{1,0:T(8,128)} %delay.1) | copy-start | bytes 9220
  0.7 208.4 %copy-start.4 = (f32[6,6,128]{2,1,0:T(8,128)S(1)}, f32[6,6,128]{2,1,0:T(8,128)}, u32[]{:S(2)}) copy-start(f32[6,6,128]{2,1,0:T(8,128)} %mmap_in.1) | copy-start | bytes 55300
  0.8 208.4 %copy-start.10 = (s32[2,128]{1,0:T(2,128)S(1)}, s32[2,128]{1,0:T(2,128)}, u32[]{:S(2)}) copy-start(s32[2,128]{1,0:T(2,128)} %param.23) | copy-start | bytes 3076
  0.8 208.4 %copy-start.12 = (s32[32,8]{0,1:T(8,128)S(1)}, s32[32,8]{0,1:T(8,128)}, u32[]{:S(2)}) copy-start(s32[32,8]{0,1:T(8,128)} %param.22) | copy-start | bytes 3076
  0.8 208.4 %copy-start.11 = (s32[32]{0:T(128)S(1)}, s32[32]{0:T(128)}, u32[]{:S(2)}) copy-start(s32[32]{0:T(128)} %counts.1) | copy-start | bytes 388
